TPU v7x, 32 devices: a whole 2x2x4 slice. The times are simulated.
32 devices in a mesh: subj: 2 (over x), ha: 8 (over z, y), dev: 2 (over core).
Axes of the slice: x: 2, y: 2, z: 4, core: 2. Of those that a mesh axis runs over, the one named last changes fastest.
Arguments:
- brain_image: float32 [64, 256, 768], P('subj', 'ha', 'dev'), parts along dimension 0, may hold values from -6 to 6
- adjoint_field: float32 [64, 256, 768], P('subj', 'ha', 'dev'), parts along dimension 0, may hold values from -6 to 6
- velocity_modes: float32 [6, 16, 32, 32], P('subj'), parts along dimension 0, may hold values from -4 to 4
Outputs:
- adjoint_end: float32 [64, 256, 768], P('subj', 'ha', 'dev'), parts along dimension 0
- image_end: float32 [64, 256, 768], P('subj', 'ha', 'dev'), parts along dimension 0
- velocity_next: float32 [6, 16, 32, 32], P('subj'), parts along dimension 0
There are 2 independent parts, one for each index of `subj`. A program takes and returns all parts, laid end to end along the dimension named above; each array names one. Nothing has to cross between parts.
All inputs are finite; a program needn't handle non-finite values.
Results may differ from a plain program's by a relative error of at most 0.0003.
Values sent between devices are 32-bit elements; how exact they have to be, the bound alone decides.
No kernel may reach another device: no remote copies, remote signals or barrier semaphores. Data moves between devices by JAX's collectives and lax.ppermute only.
A program may use at most 128 MiB of HBM per device.

v0:
```python
import functools
import math

import jax
import jax.numpy as jnp
import ml_dtypes
import numpy as np
from jax import lax
from jax.experimental import pallas as pl
from jax.experimental.pallas import tpu as pltpu
from jax.sharding import PartitionSpec as P

STEPS = 4
STEP_SIZE = 4.0
STIFFNESS = 2.0
HALO = 2 * STEPS
LANES = 128
SUB = 8
F32 = jnp.float32
BF16 = jnp.bfloat16
VMEM_LIMIT = 60 * 2**20


def wavenumbers(modes):
    column = np.arange(modes)
    return np.where(column <= modes // 2, column, column - modes // 2)


def fourier_table(positions, length, modes):
    column = np.arange(modes)
    angles = (positions[:, None] * wavenumbers(modes)[None, :] % length) * (2.0 * math.pi / length)
    table = np.where(column[None, :] <= modes // 2, np.cos(angles), np.sin(angles))
    inside = (positions >= 0) & (positions < length)
    return np.where(inside[:, None], table, 0.0)


def mode_factor(planes, height, depth, modes_x, modes_yz):
    def terms(length, modes):
        eigen = 2.0 - 2.0 * np.cos(wavenumbers(modes) * (2.0 * math.pi / length))
        return eigen, np.where(np.arange(modes) == 0, length, length / 2.0)

    ex, wx = terms(planes, modes_x)
    ey, wy = terms(height, modes_yz)
    ez, wz = terms(depth, modes_yz)
    eigen = ex[:, None, None] + ey[None, :, None] + ez[None, None, :]
    norm = wx[:, None, None] * wy[None, :, None] * wz[None, None, :]
    count = modes_x * modes_yz * modes_yz
    return STEP_SIZE * math.sqrt(count) / (norm * np.square(1.0 + STIFFNESS * eigen))


def split_np(table):
    high = table.astype(np.float32).astype(ml_dtypes.bfloat16)
    low = (table - high.astype(np.float64)).astype(ml_dtypes.bfloat16)
    return high, low


class Sizes:
    def __init__(self, planes, rows, depth, modes_x, modes, count_height, count_depth):
        self.planes, self.rows, self.depth = planes, rows, depth
        self.modes_x, self.modes = modes_x, modes
        self.count_height, self.count_depth = count_height, count_depth
        self.tall = rows + 2 * HALO
        self.phases = -(-(depth + 2 * HALO) // LANES)
        self.wide = self.phases * LANES
        self.groups = planes // SUB
        self.tiles = depth // LANES
        self.packs = LANES // modes
        self.pairs = modes_x * modes
        self.chunk = self.pairs // self.packs
        assert planes % SUB == 0 and depth % LANES == 0 and rows % HALO == 0
        assert self.packs == 4 and self.wide >= depth + 2 * HALO

    def tables(self):
        n = self
        order_x = np.array([n.groups * s + g for g in range(n.groups) for s in range(SUB)])
        order_z = np.array([n.phases * l + s for s in range(n.phases) for l in range(LANES)])
        table_x = fourier_table(order_x, n.planes, n.modes_x)
        height, depth = n.rows * n.count_height, n.depth * n.count_depth
        bx = np.repeat(table_x, n.modes, axis=1) / math.sqrt(n.pairs * n.modes)
        by, by_t, bz_e, bz_p = [], [], [], []
        for i in range(n.count_height):
            table_y = fourier_table(np.arange(n.tall) - HALO + i * n.rows, height, n.modes)
            by.append(np.tile(table_y, (1, n.modes_x)))
            own = table_y[HALO : HALO + n.rows]
            by_t.append(np.repeat(own.T, n.planes, axis=1))
        bx_t = np.tile(table_x.T, (1, n.rows))
        for i in range(n.count_depth):
            place = order_z - HALO
            reach = (place >= -HALO) & (place < n.depth + HALO)
            table_z = fourier_table(place + i * n.depth, depth, n.modes) * reach[:, None]
            high, low = split_np(table_z.T)
            bz_e.append(np.concatenate([high, high, low, np.zeros_like(low)]))
            own = ((place >= 0) & (place < n.depth))[:, None]
            high, low = split_np(0.5 * table_z * own)
            held = np.zeros((3, n.wide, 2 * LANES), ml_dtypes.bfloat16)
            for c in range(3):
                held[c, :, n.modes * c : n.modes * (c + 1)] = high
                held[c, :, LANES + n.modes * c : LANES + n.modes * (c + 1)] = low
            bz_p.append(held)
        spread = np.zeros((n.depth + LANES, n.wide), ml_dtypes.bfloat16)
        for column, position in enumerate(order_z):
            z = position - HALO
            if 0 <= z < n.depth:
                spread[z, column] = 1
            elif -HALO <= z < 0:
                spread[n.depth + LANES + z, column] = 1
            elif n.depth <= z < n.depth + HALO:
                spread[z, column] = 1
        gather = np.ascontiguousarray(spread[: n.depth].T)
        factor = mode_factor(n.planes, height, depth, n.modes_x, n.modes)
        factor = factor.reshape(n.packs, n.chunk, n.modes).transpose(1, 0, 2).reshape(n.chunk, LANES)
        return dict(
            bx=bx.astype(np.float32),
            by=np.stack(by).astype(np.float32),
            bx_t=bx_t.astype(np.float32),
            by_t=np.stack(by_t).astype(np.float32),
            bz_e=np.stack(bz_e),
            bz_p=np.stack(bz_p),
            spread=spread,
            gather=gather,
            factor=factor.astype(np.float32),
        )


def split(value):
    high = value.astype(BF16)
    return high, (value - high.astype(F32)).astype(BF16)


def dot(a, b):
    return jnp.dot(a, b, preferred_element_type=F32)


def unpacked(packed, c, n):
    lane = lax.broadcasted_iota(jnp.int32, (n.chunk, LANES), 1) // n.modes
    piece = packed[c * n.chunk : (c + 1) * n.chunk]
    parts = []
    for g in range(n.packs):
        held = jnp.where(lane == g, piece, 0.0)
        held = held + pltpu.roll(held, n.modes, 1)
        parts.append(held + pltpu.roll(held, 2 * n.modes, 1))
    return jnp.concatenate(parts, axis=0)


def expand_into(n, coeffs, w_ref, bx_ref, by_ref, bz_ref, speed):
    for c in range(3):
        high, low = split(coeffs[c])
        w_ref[:, c * LANES : (c + 1) * LANES] = high
        w_ref[:, (3 + c) * LANES : (4 + c) * LANES] = low
    chunk = SUB
    lane = lax.broadcasted_iota(jnp.int32, (chunk * n.planes, LANES), 1) // n.modes

    def body(i, _):
        rows = pl.ds(pl.multiple_of(i * chunk, chunk), chunk)
        by = by_ref[rows, :]
        bx = bx_ref[...]
        table = jnp.concatenate([bx * by[j : j + 1, :] for j in range(chunk)], axis=0)
        high, low = split(table)
        main = dot(high, w_ref[...])
        rest = dot(low, w_ref[:, : 3 * LANES])
        size = None
        for c in range(3):
            inner = (
                main[:, c * LANES : (c + 1) * LANES]
                + main[:, (3 + c) * LANES : (4 + c) * LANES]
                + rest[:, c * LANES : (c + 1) * LANES]
            )
            head = inner.astype(BF16).astype(F32)
            mixed = jnp.where(lane == 1, inner - head, head).astype(BF16)
            full = dot(mixed, bz_ref[...])
            size = jnp.abs(full) if c == 0 else size + jnp.abs(full)
            for s in range(n.phases):
                part = full[:, s * LANES : (s + 1) * LANES]
                speed[c, rows, s] = part.reshape(chunk, n.groups, SUB, LANES)
        for s in range(n.phases):
            part = 1.0 - size[:, s * LANES : (s + 1) * LANES]
            speed[3, rows, s] = part.reshape(chunk, n.groups, SUB, LANES)
        return 0

    lax.fori_loop(0, n.tall // chunk, body, 0)


def field_copies(n, own, low, high, side, side_low, side_high, raw, sems):
    count = n.planes * n.rows
    thin = n.planes * HALO
    jobs = []
    for t in range(n.tiles):
        cut = slice(t * LANES, (t + 1) * LANES)
        jobs.append((own.at[:, cut], raw.at[t, 0:count]))
        jobs.append((low.at[:, cut], raw.at[t, count : count + thin]))
        jobs.append((high.at[:, cut], raw.at[t, count + thin : count + 2 * thin]))
    jobs.append((side, raw.at[n.tiles, 0:count]))
    jobs.append((side_low, raw.at[n.tiles, count : count + thin]))
    jobs.append((side_high, raw.at[n.tiles, count + thin : count + 2 * thin]))
    return [pltpu.make_async_copy(a, b, sems.at[i]) for i, (a, b) in enumerate(jobs)]


def interleave(n, raw, spread, field):
    count = n.planes * n.rows
    thin = n.planes * HALO

    def chunk(first, base, rows, y_of, target):
        columns = []
        for t in range(n.tiles + 1):
            blocks = []
            for j in range(HALO):
                for g in range(n.groups):
                    start = base + g * rows + y_of + j
                    blocks.append(raw[t, pl.ds(start, SUB, stride=n.groups * rows), :])
            columns.append(jnp.concatenate(blocks, axis=0))
        value = jnp.concatenate(columns, axis=1)
        high, low = split(value)
        out = dot(high, spread[...]) + dot(low, spread[...])
        for s in range(n.phases):
            part = out[:, s * LANES : (s + 1) * LANES]
            field[target, s] = part.reshape(HALO, n.groups, SUB, LANES)

    chunk(0, count, HALO, 0, slice(0, HALO))
    chunk(0, count + thin, HALO, 0, slice(HALO + n.rows, 2 * HALO + n.rows))

    def body(i, _):
        y = pl.multiple_of(i * HALO, HALO)
        chunk(0, 0, n.rows, y, pl.ds(y + HALO, HALO))
        return 0

    lax.fori_loop(0, n.rows // HALO, body, 0)


def neighbours(n, field, y0, rows):
    held = {}
    sub = lax.broadcasted_iota(jnp.int32, (SUB, LANES), 0)
    first, last = sub == 0, sub == SUB - 1
    phases, groups = n.phases, n.groups

    def at(j, s, g):
        if (j, s, g) not in held:
            held[j, s, g] = field[y0 + j, s, g]
        return held[j, s, g]

    edges = {}
    for j in range(rows):
        for g in range(groups):
            edges["zp", j, g] = pltpu.roll(at(j, 0, g), LANES - 1, 1)
            edges["zm", j, g] = pltpu.roll(at(j, phases - 1, g), 1, 1)
        for s in range(phases):
            edges["xp", j, s] = jnp.where(last, 0.0, pltpu.roll(at(j, s, 0), SUB - 1, 0))
            edges["xm", j, s] = jnp.where(first, 0.0, pltpu.roll(at(j, s, groups - 1), 1, 0))

    def around(j, s, g):
        xm = at(j, s, g - 1) if g else edges["xm", j, s]
        xp = at(j, s, g + 1) if g < groups - 1 else edges["xp", j, s]
        zm = at(j, s - 1, g) if s else edges["zm", j, g]
        zp = at(j, s + 1, g) if s < phases - 1 else edges["zp", j, g]
        return at(j, s, g), (xm, at(j - 1, s, g), zm), (xp, at(j + 1, s, g), zp)

    return around


def upwind_rows(n, source, target, speed, y0, rows, second):
    around = neighbours(n, source, y0, rows)
    for j in range(rows):
        for s in range(n.phases):
            for g in range(n.groups):
                here, behind, ahead = around(j, s, g)
                total = speed[3, y0 + j, s, g] * here
                for d in range(3):
                    u = speed[d, y0 + j, s, g]
                    total = total + jnp.abs(u) * jnp.where(u > 0, behind[d], ahead[d])
                if second:
                    total = 0.5 * (target[y0 + j, s, g] + total)
                target[y0 + j, s, g] = total


def sweep(n, source, target, speed, low, high, second):
    count = (high - low) // 4
    lax.fori_loop(
        0,
        count,
        lambda i, _: (upwind_rows(n, source, target, speed, low + 4 * i, 4, second), 0)[1],
        0,
    )
    return low + 4 * count


def transport(n, field, spare, speed):
    tall = n.tall

    def step(r, _):
        first = 2 * r + 1
        done = sweep(n, field, spare, speed, first, tall - first, False)
        if (tall - 2) % 4:
            upwind_rows(n, field, spare, speed, done, 2, False)
        done = sweep(n, spare, field, speed, first + 1, tall - first - 1, True)
        if tall % 4:
            upwind_rows(n, spare, field, speed, done, 2, True)
        return 0

    lax.fori_loop(0, STEPS, step, 0)


def deinterleave(n, field, gather, out):
    def body(i, _):
        y = pl.multiple_of(i * HALO, HALO)
        columns = [
            field[pl.ds(y + HALO, HALO), s].reshape(HALO * n.planes, LANES) for s in range(n.phases)
        ]
        high, low = split(jnp.concatenate(columns, axis=1))
        value = dot(high, gather[...]) + dot(low, gather[...])
        for t in range(n.tiles):
            for j in range(HALO):
                for g in range(n.groups):
                    row = j * n.planes + g * SUB
                    out[t, pl.ds(g * n.rows + y + j, SUB, stride=n.groups * n.rows), :] = value[
                        row : row + SUB, t * LANES : (t + 1) * LANES
                    ]
        return 0

    lax.fori_loop(0, n.rows // HALO, body, 0)


def result_copies(n, out, target, sems):
    return [
        pltpu.make_async_copy(out.at[t], target.at[:, t * LANES : (t + 1) * LANES], sems.at[t])
        for t in range(n.tiles)
    ]


def force(n, adjoint, image, f_high, f_low):
    def body(y, _):
        around = neighbours(n, image, y + HALO, 1)
        for s in range(n.phases):
            pieces = [[], [], []]
            for g in range(n.groups):
                _, behind, ahead = around(0, s, g)
                end = adjoint[y + HALO, s, g]
                for d in range(3):
                    pieces[d].append(end * (ahead[d] - behind[d]))
            for d in range(3):
                high, low = split(jnp.concatenate(pieces[d], axis=0))
                rows = pl.ds(pl.multiple_of(y * n.planes, n.planes), n.planes)
                f_high[d, rows, s * LANES : (s + 1) * LANES] = high
                f_low[d, rows, s * LANES : (s + 1) * LANES] = low
        return 0

    lax.fori_loop(0, n.rows, body, 0)


def project(n, f_high, f_low, bz_ref, bx_ref, by_ref, total, packed):
    size = HALO * n.planes
    total[...] = jnp.zeros_like(total)

    def body(i, _):
        start = pl.multiple_of(i * size, size)
        rows = pl.ds(start, size)
        main, rest = None, None
        for d in range(3):
            one = dot(f_high[d, rows, :], bz_ref[d])
            two = dot(f_low[d, rows, :], bz_ref[d, :, :LANES])
            main = one if d == 0 else main + one
            rest = two if d == 0 else rest + two
        inner = main[:, :LANES] + main[:, LANES:] + rest
        high, low = split(inner)
        by = by_ref[:, rows]
        bx = bx_ref[:, rows]
        table = jnp.concatenate([by * bx[a : a + 1, :] for a in range(n.modes_x)], axis=0)
        t_high, t_low = split(table)
        both = dot(t_high, jnp.concatenate([high, low], axis=1))
        total[...] += both[:, :LANES] + both[:, LANES:] + dot(t_low, high)
        return 0

    lax.fori_loop(0, n.rows // HALO, body, 0)
    lane = lax.broadcasted_iota(jnp.int32, (n.chunk, LANES), 1) // n.modes
    for c in range(3):
        value = jnp.zeros((n.chunk, LANES), F32)
        for g in range(n.packs):
            piece = total[g * n.chunk : (g + 1) * n.chunk, :]
            shift = (n.modes * (g - c)) % LANES
            value = jnp.where(lane == g, pltpu.roll(piece, shift, 1) if shift else piece, value)
        packed[c * n.chunk : (c + 1) * n.chunk, :] = value


def first_kernel(n, _, modes, bx, by, bz_e, bz_p, bx_t, by_t, spread, gather, *rest):
    fields, rest = rest[:12], rest[12:]
    packed, end, speed, field, spare, image, raw_a, raw_b, w, f_high, f_low, total, sems = rest
    pulls_a = field_copies(n, *fields[:6], raw_a, sems.at[0])
    pulls_b = field_copies(n, *fields[6:], raw_b, sems.at[1])
    for copy in pulls_a + pulls_b:
        copy.start()
    coeffs = [-unpacked(modes[...], c, n) for c in range(3)]
    expand_into(n, coeffs, w, bx, by.at[0], bz_e.at[0], speed)
    for copy in pulls_a:
        copy.wait()
    interleave(n, raw_a, spread, field)
    transport(n, field, spare, speed)
    for copy in pulls_b:
        copy.wait()
    interleave(n, raw_b, spread, image)
    deinterleave(n, field, gather, raw_a.at[:, : n.planes * n.rows])
    pushes = result_copies(n, raw_a.at[:, : n.planes * n.rows], end, sems.at[2])
    for copy in pushes:
        copy.start()
    force(n, field, image, f_high, f_low)
    project(n, f_high, f_low, bz_p.at[0], bx_t, by_t.at[0], total, packed)
    for copy in pushes:
        copy.wait()


def second_kernel(n, _, modes, summed, factor, bx, by, bz_e, spread, gather, *rest):
    fields, rest = rest[:6], rest[6:]
    end, updated, speed, field, spare, raw, w, sems = rest
    pulls = field_copies(n, *fields, raw, sems.at[0])
    for copy in pulls:
        copy.start()
    scale = jnp.concatenate([factor[...]] * 3, axis=0)
    packed = modes[...] + scale * summed[...]
    coeffs = [unpacked(packed, c, n) for c in range(3)]
    for c in range(3):
        updated[c] = coeffs[c][:, : n.modes]
    expand_into(n, coeffs, w, bx, by.at[0], bz_e.at[0], speed)
    for copy in pulls:
        copy.wait()
    interleave(n, raw, spread, field)
    transport(n, field, spare, speed)
    deinterleave(n, field, gather, raw.at[:, : n.planes * n.rows])
    pushes = result_copies(n, raw.at[:, : n.planes * n.rows], end, sems.at[1])
    for copy in pushes:
        copy.start()
    for copy in pushes:
        copy.wait()


def swap_with(value, axis, step):
    count = lax.axis_size(axis)
    return lax.ppermute(value, axis, [(i, i ^ step) for i in range(count)])


def sum_over_devices(packed):
    count_height, count_depth = lax.axis_size("ha"), lax.axis_size("dev")
    if count_depth != 2 or count_height & (count_height - 1):
        return lax.psum(packed, ("ha", "dev"))
    halves = packed.reshape(2, -1, LANES)
    side = lax.axis_index("dev")
    kept = lax.dynamic_index_in_dim(halves, side, 0, False)
    given = lax.dynamic_index_in_dim(halves, 1 - side, 0, False)
    kept = kept + swap_with(given, "dev", 1)
    step = 1
    while step < count_height:
        kept = kept + swap_with(kept, "ha", step)
        step *= 2
    other = swap_with(kept, "dev", 1)
    first = jnp.where(side == 0, kept, other)
    second = jnp.where(side == 0, other, kept)
    return jnp.concatenate([first, second], axis=0)


def beside(cells):
    count = lax.axis_size("dev")
    index = lax.axis_index("dev")
    lane = lax.broadcasted_iota(jnp.int32, (1, 1, LANES), 2)
    head = jnp.where(lane < LANES // 2, cells[:, :, :LANES], 0.0)
    tail = jnp.where(lane >= LANES // 2, cells[:, :, -LANES:], 0.0)
    if count == 1:
        return jnp.zeros_like(head)
    if count == 2:
        return swap_with(jnp.where(index == 0, tail, head), "dev", 1)
    ends = range(count - 1)
    return lax.ppermute(tail, "dev", [(i, i + 1) for i in ends]) + lax.ppermute(
        head, "dev", [(i + 1, i) for i in ends]
    )


def with_halos(cells):
    ends = range(lax.axis_size("ha") - 1)
    low = lax.ppermute(cells[:, -HALO:], "ha", [(i, i + 1) for i in ends])
    high = lax.ppermute(cells[:, :HALO], "ha", [(i + 1, i) for i in ends])
    side = beside(cells)
    both = beside(jnp.concatenate([low, high], axis=1))
    parts = (cells, low, high, side, both[:, :HALO], both[:, HALO:])
    return [part.reshape(-1, part.shape[-1]) for part in parts]


def per_device(brain_image, adjoint_field, velocity_modes):
    planes, rows, depth = brain_image.shape
    n = Sizes(
        planes,
        rows,
        depth,
        velocity_modes.shape[1],
        velocity_modes.shape[2],
        lax.axis_size("ha"),
        lax.axis_size("dev"),
    )
    t = {name: jnp.asarray(value) for name, value in n.tables().items()}
    place = jnp.stack([lax.axis_index("ha"), lax.axis_index("dev")]).astype(jnp.int32)
    modes = velocity_modes.reshape(3, n.packs, n.chunk, n.modes).transpose(0, 2, 1, 3)
    modes = modes.reshape(3 * n.chunk, LANES)
    adjoint = with_halos(adjoint_field)
    image = with_halos(brain_image)

    whole = pl.BlockSpec(memory_space=pltpu.VMEM)
    outside = pl.BlockSpec(memory_space=pl.ANY)

    def picked(table, axis):
        zeros = (0,) * (table.ndim - 1)
        return pl.BlockSpec((1,) + table.shape[1:], lambda i, at: (at[axis],) + zeros)

    block = (n.tall, n.phases, n.groups, SUB, LANES)
    raw = pltpu.VMEM((n.tiles + 1, planes * n.tall, LANES), F32)
    pulls = 3 * n.tiles + 3
    packed_shape = (3 * n.chunk, LANES)
    flat = (planes * rows, depth)
    params = pltpu.CompilerParams(vmem_limit_bytes=VMEM_LIMIT)
    packed, adjoint_end = pl.pallas_call(
        functools.partial(first_kernel, n),
        grid_spec=pltpu.PrefetchScalarGridSpec(
            num_scalar_prefetch=1,
            grid=(1,),
            in_specs=[
                whole, whole, picked(t["by"], 0), picked(t["bz_e"], 1), picked(t["bz_p"], 1),
                whole, picked(t["by_t"], 0), whole, whole,
            ] + [outside] * 12,
            out_specs=[whole, outside],
            scratch_shapes=[
                pltpu.VMEM((4,) + block, F32),
                pltpu.VMEM(block, F32),
                pltpu.VMEM(block, F32),
                pltpu.VMEM(block, F32),
                raw,
                raw,
                pltpu.VMEM((n.pairs, 6 * LANES), BF16),
                pltpu.VMEM((3, planes * rows, n.wide), BF16),
                pltpu.VMEM((3, planes * rows, n.wide), BF16),
                pltpu.VMEM((n.pairs, LANES), F32),
                pltpu.SemaphoreType.DMA((3, pulls)),
            ],
        ),
        out_shape=[jax.ShapeDtypeStruct(packed_shape, F32), jax.ShapeDtypeStruct(flat, F32)],
        compiler_params=params,
    )(
        place, modes, t["bx"], t["by"], t["bz_e"], t["bz_p"], t["bx_t"], t["by_t"], t["spread"],
        t["gather"], *adjoint, *image,
    )
    summed = sum_over_devices(packed)
    image_end, updated = pl.pallas_call(
        functools.partial(second_kernel, n),
        grid_spec=pltpu.PrefetchScalarGridSpec(
            num_scalar_prefetch=1,
            grid=(1,),
            in_specs=[
                whole, whole, whole, whole, picked(t["by"], 0), picked(t["bz_e"], 1), whole, whole,
            ] + [outside] * 6,
            out_specs=[outside, whole],
            scratch_shapes=[
                pltpu.VMEM((4,) + block, F32),
                pltpu.VMEM(block, F32),
                pltpu.VMEM(block, F32),
                raw,
                pltpu.VMEM((n.pairs, 6 * LANES), BF16),
                pltpu.SemaphoreType.DMA((2, pulls)),
            ],
        ),
        out_shape=[
            jax.ShapeDtypeStruct(flat, F32),
            jax.ShapeDtypeStruct((3, n.pairs, n.modes), F32),
        ],
        compiler_params=params,
    )(place, modes, summed, t["factor"], t["bx"], t["by"], t["bz_e"], t["spread"], t["gather"], *image)
    return (
        adjoint_end.reshape(brain_image.shape),
        image_end.reshape(brain_image.shape),
        updated.reshape(velocity_modes.shape),
    )


def solution(mesh):
    placed = (P("subj", "ha", "dev"), P("subj", "ha", "dev"), P("subj", None, None, None))
    return jax.shard_map(
        per_device,
        mesh=mesh,
        in_specs=placed,
        out_specs=placed,
        check_vma=False,
    )
```

profile of v0, /device:TPU:25, one launch (start us, length us, event | category | flops | bytes accessed | tf_op | source)
XLA Modules:
  0.0 141.6 jit_solution(9985197187668082884)
XLA Ops:
  0.6 0.0 copy-start.1
  0.6 1.3 fusion.2
  1.9 3.1 %collective-permute-start.4 = (f32[32,8,384]{2,1,0:T(8,128)S(1)}, f32[32,8,384]{2,1,0:T(8,128)S(1)}, u32[]{:S(2)}, u32[]{:S(2)}) collective-permute-start(f32[32,8,384]{2,1,0:T(8,128)S(1)} %get-tuple-element.12), channel_id=1, source_target_pairs={{0,2},{2,4},{4,6},{6,8},{8,10},{10,12},{12,14},{1,3},{3,5},{5,7},{... | collective-permute-start | bytes 1179656 | tf_op jit(solution)/shard_map/ppermute | solution.py:474
  5.1 0.0 copy-done.1
  5.1 0.8 fusion.3
  5.9 1.9 %collective-permute-start = (f32[32,8,384]{2,1,0:T(8,128)}, f32[32,8,384]{2,1,0:T(8,128)S(1)}, u32[]{:S(2)}, u32[]{:S(2)}) collective-permute-start(f32[32,8,384]{2,1,0:T(8,128)} %get-tuple-element.14), channel_id=1, source_target_pairs={{0,2},{2,4},{4,6},{6,8},{8,10},{10,12},{12,14},{1,3},{3,5},{5,7},{... | collective-permute-start | bytes 1179656 | tf_op jit(solution)/shard_map/ppermute | solution.py:474
  7.8 4.3 %collective-permute-start.5 = (f32[32,8,384]{2,1,0:T(8,128)S(1)}, f32[32,8,384]{2,1,0:T(8,128)}, u32[]{:S(2)}, u32[]{:S(2)}) collective-permute-start(f32[32,8,384]{2,1,0:T(8,128)S(1)} %get-tuple-element.11), channel_id=1, source_target_pairs={{2,0},{4,2},{6,4},{8,6},{10,8},{12,10},{14,12},{3,1},{5,3},{7,5},{... | collective-permute-start | bytes 1179656 | tf_op jit(solution)/shard_map/ppermute | solution.py:475
  12.1 2.1 %collective-permute-start.1 = (f32[32,8,384]{2,1,0:T(8,128)S(1)}, f32[32,8,384]{2,1,0:T(8,128)}, u32[]{:S(2)}, u32[]{:S(2)}) collective-permute-start(f32[32,8,384]{2,1,0:T(8,128)S(1)} %get-tuple-element.13), channel_id=1, source_target_pairs={{2,0},{4,2},{6,4},{8,6},{10,8},{12,10},{14,12},{3,1},{5,3},{7,5},{... | collective-permute-start | bytes 1179656 | tf_op jit(solution)/shard_map/ppermute | solution.py:475
  14.2 0.5 collective-permute-done.4
  14.8 0.0 copy-start.2
  14.8 8.4 %collective-permute-done = f32[32,8,384]{2,1,0:T(8,128)S(1)} collective-permute-done((f32[32,8,384]{2,1,0:T(8,128)}, f32[32,8,384]{2,1,0:T(8,128)S(1)}, u32[]{:S(2)}, u32[]{:S(2)}) %collective-permute-start) | collective-permute-done | bytes 393248 | tf_op jit(solution)/shard_map/ppermute | solution.py:474
  23.2 0.0 copy-start.4
  23.2 0.7 copy-done.4
  24.0 0.0 copy-start
  24.0 8.8 %collective-permute-done.5 = f32[32,8,384]{2,1,0:T(8,128)} collective-permute-done((f32[32,8,384]{2,1,0:T(8,128)S(1)}, f32[32,8,384]{2,1,0:T(8,128)}, u32[]{:S(2)}, u32[]{:S(2)}) %collective-permute-start.5) | collective-permute-done | bytes 393248 | tf_op jit(solution)/shard_map/ppermute | solution.py:475
  32.7 1.0 constant_dynamic-update-slice_fusion.2
  33.7 7.4 %collective-permute-done.1 = f32[32,8,384]{2,1,0:T(8,128)} collective-permute-done((f32[32,8,384]{2,1,0:T(8,128)S(1)}, f32[32,8,384]{2,1,0:T(8,128)}, u32[]{:S(2)}, u32[]{:S(2)}) %collective-permute-start.1) | collective-permute-done | bytes 393248 | tf_op jit(solution)/shard_map/ppermute | solution.py:475
  41.1 1.0 constant_dynamic-update-slice_fusion
  42.2 0.0 copy-done.2
  42.2 0.9 fusion
  43.0 0.0 copy-start.5
  43.0 0.5 collective-permute-start.7
  43.5 0.0 copy-done
  43.5 0.1 select_select_fusion
  43.7 0.1 collective-permute-start.6
  43.8 0.5 collective-permute-start.2
  44.3 0.1 collective-permute-start.3
  44.3 0.7 pad_add_fusion._
  45.0 0.0 copy-done.5
  45.0 0.3 copy.16
  45.4 0.8 copy.17.modes
  46.2 0.0 collective-permute-done.7
  46.2 1.7 %slice_bitcast_fusion = (f32[256,128]{1,0:T(8,128)}, f32[256,128]{1,0:T(8,128)}) fusion(f32[32,16,128]{2,1,0:T(8,128)} %collective-permute-done.7), kind=kLoop, calls=%fused_computation.10 | loop fusion | bytes 524288 | tf_op jit(solution)/shard_map/reshape | solution.py:479
  47.9 0.0 collective-permute-done.3
  47.9 1.7 %slice_bitcast_fusion.2 = (f32[256,128]{1,0:T(8,128)}, f32[256,128]{1,0:T(8,128)}) fusion(f32[32,16,128]{2,1,0:T(8,128)} %collective-permute-done.3), kind=kLoop, calls=%fused_computation.12 | loop fusion | bytes 524288 | tf_op jit(solution)/shard_map/reshape | solution.py:479
  49.6 0.0 collective-permute-done.6
  49.6 0.0 copy-start.3
  49.6 0.0 collective-permute-done.2
  49.6 0.0 copy-start.6
  49.6 0.8 copy-done.3
  50.4 0.2 copy-done.6
  50.5 39.4 %shard_map.139 = (f32[384,128]{1,0:T(8,128)}, f32[1024,384]{1,0:T(8,128)}) custom-call(s32[2]{0:T(128)} %pad_add_fusion._, f32[384,128]{1,0:T(8,128)} %copy.17.modes, f32[32,512]{1,0:T(8,128)} %constant.43.clone.bx, f32[8,48,512]{2,1,0:T(8,128)} %constant.44.clone.by, bf16[2,128,512]{2,1,0:T(8,128)(2,1)} %constant.47.clone.bz_e, ...), custom_call_target="tpu_custom_call" | custom-call | tf_op jit(solution)/shard_map/pallas_call | solution.py:513
  89.9 0.9 dynamic-slice_bitcast_fusion
  90.8 0.4 collective-permute-start.8
  91.3 0.9 collective-permute-done.8
  92.2 0.9 bitcast_add_fusion
  93.1 0.1 collective-permute-start.9
  93.2 4.0 %collective-permute-done.9 = f32[192,128]{1,0:T(8,128)S(1)} collective-permute-done((f32[192,128]{1,0:T(8,128)S(1)}, f32[192,128]{1,0:T(8,128)S(1)}, u32[]{:S(2)}, u32[]{:S(2)}) %collective-permute-start.9) | collective-permute-done | bytes 98336 | tf_op jit(solution)/shard_map/ppermute | solution.py:434
  97.2 1.3 collective-permute-start.10
  98.5 2.2 %collective-permute-done.10 = f32[192,128]{1,0:T(8,128)S(1)} collective-permute-done((f32[192,128]{1,0:T(8,128)S(1)}, f32[192,128]{1,0:T(8,128)S(1)}, u32[]{:S(2)}, u32[]{:S(2)}) %collective-permute-start.10) | collective-permute-done | bytes 98336 | tf_op jit(solution)/shard_map/ppermute | solution.py:434
  100.8 1.2 collective-permute-start.11
  102.0 4.3 %collective-permute-done.11 = f32[192,128]{1,0:T(8,128)S(1)} collective-permute-done((f32[192,128]{1,0:T(8,128)S(1)}, f32[192,128]{1,0:T(8,128)S(1)}, u32[]{:S(2)}, u32[]{:S(2)}) %collective-permute-start.11) | collective-permute-done | bytes 98336 | tf_op jit(solution)/shard_map/ppermute | solution.py:434
  106.3 3.5 %collective-permute-start.12 = (f32[192,128]{1,0:T(8,128)S(1)}, f32[192,128]{1,0:T(8,128)S(1)}, u32[]{:S(2)}, u32[]{:S(2)}) collective-permute-start(f32[192,128]{1,0:T(8,128)S(1)} %add.25), channel_id=1, source_target_pairs={{0,1},{1,0},{2,3},{3,2},{4,5},{5,4},{6,7},{7,6},{8,9},{9,8},{10,11... | collective-permute-start | bytes 294920 | tf_op jit(solution)/shard_map/ppermute | solution.py:434
  109.8 0.9 collective-permute-done.12
  110.8 0.7 pad_maximum_fusion.summed
  111.5 30.1 %shard_map.140 = (f32[1024,384]{1,0:T(8,128)}, f32[3,512,32]{2,1,0:T(8,128)}) custom-call(s32[2]{0:T(128)} %pad_add_fusion._, f32[384,128]{1,0:T(8,128)} %copy.17.modes, f32[384,128]{1,0:T(8,128)} %pad_maximum_fusion.summed, f32[128,128]{1,0:T(8,128)} %constant.51.clone.factor, f32[32,512]{1,0:T(8,128)} %constant.43.clone.bx, ...), custom_call_target="tpu_custom_call" | custom-call | tf_op jit(solution)/shard_map/pallas_call | solution.py:544
  (8 shorter events, 0.1 us)
Async XLA Ops:
  0.6 4.5 %copy-start.1 = (f32[32,32,384]{2,1,0:T(8,128)S(1)}, f32[32,32,384]{2,1,0:T(8,128)}, u32[]{:S(2)}) copy-start(f32[32,32,384]{2,1,0:T(8,128)} %param.13) | copy-start | bytes 4718596
  1.9 12.8 %collective-permute-start.4 = (f32[32,8,384]{2,1,0:T(8,128)S(1)}, f32[32,8,384]{2,1,0:T(8,128)S(1)}, u32[]{:S(2)}, u32[]{:S(2)}) collective-permute-start(f32[32,8,384]{2,1,0:T(8,128)S(1)} %get-tuple-element.12), channel_id=1, source_target_pairs={{0,2},{2,4},{4,6},{6,8},{8,10},{10,12},{12,14},{1,3},{3,5},{5,7},{... | collective-permute-start | bytes 1179656 | tf_op jit(solution)/shard_map/ppermute | solution.py:474
  5.9 17.3 %collective-permute-start = (f32[32,8,384]{2,1,0:T(8,128)}, f32[32,8,384]{2,1,0:T(8,128)S(1)}, u32[]{:S(2)}, u32[]{:S(2)}) collective-permute-start(f32[32,8,384]{2,1,0:T(8,128)} %get-tuple-element.14), channel_id=1, source_target_pairs={{0,2},{2,4},{4,6},{6,8},{8,10},{10,12},{12,14},{1,3},{3,5},{5,7},{... | collective-permute-start | bytes 1179656 | tf_op jit(solution)/shard_map/ppermute | solution.py:474
  7.8 24.9 %collective-permute-start.5 = (f32[32,8,384]{2,1,0:T(8,128)S(1)}, f32[32,8,384]{2,1,0:T(8,128)}, u32[]{:S(2)}, u32[]{:S(2)}) collective-permute-start(f32[32,8,384]{2,1,0:T(8,128)S(1)} %get-tuple-element.11), channel_id=1, source_target_pairs={{2,0},{4,2},{6,4},{8,6},{10,8},{12,10},{14,12},{3,1},{5,3},{7,5},{... | collective-permute-start | bytes 1179656 | tf_op jit(solution)/shard_map/ppermute | solution.py:475
  12.1 29.1 %collective-permute-start.1 = (f32[32,8,384]{2,1,0:T(8,128)S(1)}, f32[32,8,384]{2,1,0:T(8,128)}, u32[]{:S(2)}, u32[]{:S(2)}) collective-permute-start(f32[32,8,384]{2,1,0:T(8,128)S(1)} %get-tuple-element.13), channel_id=1, source_target_pairs={{2,0},{4,2},{6,4},{8,6},{10,8},{12,10},{14,12},{3,1},{5,3},{7,5},{... | collective-permute-start | bytes 1179656 | tf_op jit(solution)/shard_map/ppermute | solution.py:475
  14.8 27.4 %copy-start.2 = (f32[32,8,384]{2,1,0:T(8,128)}, f32[32,8,384]{2,1,0:T(8,128)S(1)}, u32[]{:S(2)}) copy-start(f32[32,8,384]{2,1,0:T(8,128)S(1)} %collective-permute-done.4) | copy-start | bytes 1179652
  23.2 0.7 copy-start.4
  24.0 19.6 %copy-start = (f32[32,32,384]{2,1,0:T(8,128)S(1)}, f32[32,32,384]{2,1,0:T(8,128)}, u32[]{:S(2)}) copy-start(f32[32,32,384]{2,1,0:T(8,128)} %param.12) | copy-start | bytes 4718596
  43.0 2.0 %copy-start.5 = (f32[3,16,32,32]{3,2,1,0:T(8,128)S(1)}, f32[3,16,32,32]{3,2,1,0:T(8,128)}, u32[]{:S(2)}) copy-start(f32[3,16,32,32]{3,2,1,0:T(8,128)} %param.14) | copy-start | bytes 589828
  43.0 3.1 %collective-permute-start.7 = (f32[32,16,128]{2,1,0:T(8,128)}, f32[32,16,128]{2,1,0:T(8,128)}, u32[]{:S(2)}, u32[]{:S(2)}) collective-permute-start(f32[32,16,128]{2,1,0:T(8,128)} %get-tuple-element.21), channel_id=1, source_target_pairs={{0,1},{1,0},{2,3},{3,2},{4,5},{5,4},{6,7},{7,6},{8,9},{9,8},{10,11... | collective-permute-start | bytes 786440 | tf_op jit(solution)/shard_map/ppermute | solution.py:434
  43.7 5.9 %collective-permute-start.6 = (f32[32,32,128]{2,1,0:T(8,128)S(1)}, f32[32,32,128]{2,1,0:T(8,128)S(1)}, u32[]{:S(2)}, u32[]{:S(2)}) collective-permute-start(f32[32,32,128]{2,1,0:T(8,128)S(1)} %get-tuple-element.23), channel_id=1, source_target_pairs={{0,1},{1,0},{2,3},{3,2},{4,5},{5,4},{6,7},{7,6},{8,9},{9,8},{10,11... | collective-permute-start | bytes 1572872 | tf_op jit(solution)/shard_map/ppermute | solution.py:434
  43.8 5.8 %collective-permute-start.2 = (f32[32,32,128]{2,1,0:T(8,128)S(1)}, f32[32,32,128]{2,1,0:T(8,128)S(1)}, u32[]{:S(2)}, u32[]{:S(2)}) collective-permute-start(f32[32,32,128]{2,1,0:T(8,128)S(1)} %get-tuple-element.24), channel_id=1, source_target_pairs={{0,1},{1,0},{2,3},{3,2},{4,5},{5,4},{6,7},{7,6},{8,9},{9,8},{10,11... | collective-permute-start | bytes 1572872 | tf_op jit(solution)/shard_map/ppermute | solution.py:434
  44.3 3.6 %collective-permute-start.3 = (f32[32,16,128]{2,1,0:T(8,128)}, f32[32,16,128]{2,1,0:T(8,128)}, u32[]{:S(2)}, u32[]{:S(2)}) collective-permute-start(f32[32,16,128]{2,1,0:T(8,128)} %get-tuple-element.22), channel_id=1, source_target_pairs={{0,1},{1,0},{2,3},{3,2},{4,5},{5,4},{6,7},{7,6},{8,9},{9,8},{10,11... | collective-permute-start | bytes 786440 | tf_op jit(solution)/shard_map/ppermute | solution.py:434
  49.6 0.8 copy-start.3
  49.6 1.0 copy-start.6
  90.8 1.4 collective-permute-start.8
  93.1 4.1 %collective-permute-start.9 = (f32[192,128]{1,0:T(8,128)S(1)}, f32[192,128]{1,0:T(8,128)S(1)}, u32[]{:S(2)}, u32[]{:S(2)}) collective-permute-start(f32[192,128]{1,0:T(8,128)S(1)} %bitcast_add_fusion), channel_id=1, source_target_pairs={{0,2},{2,0},{4,6},{6,4},{8,10},{10,8},{12,14},{14,12},{1,3},{3,1},... | collective-permute-start | bytes 294920 | tf_op jit(solution)/shard_map/ppermute | solution.py:434
  97.2 3.5 %collective-permute-start.10 = (f32[192,128]{1,0:T(8,128)S(1)}, f32[192,128]{1,0:T(8,128)S(1)}, u32[]{:S(2)}, u32[]{:S(2)}) collective-permute-start(f32[192,128]{1,0:T(8,128)S(1)} %add.23), channel_id=1, source_target_pairs={{0,4},{2,6},{4,0},{6,2},{8,12},{10,14},{12,8},{14,10},{1,5},{3,7},... | collective-permute-start | bytes 294920 | tf_op jit(solution)/shard_map/ppermute | solution.py:434
  100.8 5.5 %collective-permute-start.11 = (f32[192,128]{1,0:T(8,128)S(1)}, f32[192,128]{1,0:T(8,128)S(1)}, u32[]{:S(2)}, u32[]{:S(2)}) collective-permute-start(f32[192,128]{1,0:T(8,128)S(1)} %add.24), channel_id=1, source_target_pairs={{0,8},{2,10},{4,12},{6,14},{8,0},{10,2},{12,4},{14,6},{1,9},{3,11}... | collective-permute-start | bytes 294920 | tf_op jit(solution)/shard_map/ppermute | solution.py:434
  106.3 4.5 %collective-permute-start.12 = (f32[192,128]{1,0:T(8,128)S(1)}, f32[192,128]{1,0:T(8,128)S(1)}, u32[]{:S(2)}, u32[]{:S(2)}) collective-permute-start(f32[192,128]{1,0:T(8,128)S(1)} %add.25), channel_id=1, source_target_pairs={{0,1},{1,0},{2,3},{3,2},{4,5},{5,4},{6,7},{7,6},{8,9},{9,8},{10,11... | collective-permute-start | bytes 294920 | tf_op jit(solution)/shard_map/ppermute | solution.py:434
where the time goes:
time: 143 us; the launch traced here: 142 us
  Pallas kernels  69.5 us (49%)
  waiting for transfers between devices  37.5 us (26%)
  starting transfers between devices  19.1 us (13%)
  local copies, waits for them, and re-layouts  11.3 us (8%)
  other arithmetic  3.3 us (2%)
    pallas_call x1, Pallas kernels, per_device(): pl.pallas_call(functools.partial(first_kernel, n), grid_spec=pltpu.Prefet...  39.4 us
    pallas_call x1, Pallas kernels, per_device(): pl.pallas_call(functools.partial(second_kernel, n), grid_spec=pltpu.Prefe...  30.1 us
    ppermute x2, waiting for transfers between devices, with_halos(): high = lax.ppermute(cells[:, :HALO], 'ha', [(i + 1, i) for i in ends])  16.2 us
    ppermute x9, waiting for transfers between devices, swap_with(): return lax.ppermute(value, axis, [(i, i ^ step) for i in range(count)])  12.5 us
    ppermute x2, waiting for transfers between devices, with_halos(): low = lax.ppermute(cells[:, -HALO:], 'ha', [(i, i + 1) for i in ends])  8.9 us
    ppermute x9, starting transfers between devices, swap_with(): return lax.ppermute(value, axis, [(i, i ^ step) for i in range(count)])  7.65 us
    ppermute x2, starting transfers between devices, with_halos(): high = lax.ppermute(cells[:, :HALO], 'ha', [(i + 1, i) for i in ends])  6.4 us
    ppermute x2, starting transfers between devices, with_halos(): low = lax.ppermute(cells[:, -HALO:], 'ha', [(i, i + 1) for i in ends])  5.06 us
  transfers between devices with their start and end apart: 13, of which 9 were waited for; matrix products, arithmetic and copies ran while one was open for 5% of the time, Pallas kernels for 0%

commit v1 on v0

--- a/solution.py
+++ b/solution.py
@@ -18,7 +18,6 @@
 SUB = 8
 F32 = jnp.float32
 BF16 = jnp.bfloat16
-VMEM_LIMIT = 60 * 2**20
 
 
 def wavenumbers(modes):
@@ -180,50 +179,90 @@
     lax.fori_loop(0, n.tall // chunk, body, 0)
 
 
-def field_copies(n, own, low, high, side, side_low, side_high, raw, sems):
-    count = n.planes * n.rows
-    thin = n.planes * HALO
-    jobs = []
-    for t in range(n.tiles):
-        cut = slice(t * LANES, (t + 1) * LANES)
-        jobs.append((own.at[:, cut], raw.at[t, 0:count]))
-        jobs.append((low.at[:, cut], raw.at[t, count : count + thin]))
-        jobs.append((high.at[:, cut], raw.at[t, count + thin : count + 2 * thin]))
-    jobs.append((side, raw.at[n.tiles, 0:count]))
-    jobs.append((side_low, raw.at[n.tiles, count : count + thin]))
-    jobs.append((side_high, raw.at[n.tiles, count + thin : count + 2 * thin]))
+def own_copies(n, own, side, raw, sems):
+    jobs = [(own.at[:, t * LANES : (t + 1) * LANES], raw.at[t]) for t in range(n.tiles)]
+    jobs.append((side, raw.at[n.tiles]))
     return [pltpu.make_async_copy(a, b, sems.at[i]) for i, (a, b) in enumerate(jobs)]
 
 
-def interleave(n, raw, spread, field):
-    count = n.planes * n.rows
-    thin = n.planes * HALO
-
-    def chunk(first, base, rows, y_of, target):
-        columns = []
-        for t in range(n.tiles + 1):
-            blocks = []
-            for j in range(HALO):
-                for g in range(n.groups):
-                    start = base + g * rows + y_of + j
-                    blocks.append(raw[t, pl.ds(start, SUB, stride=n.groups * rows), :])
-            columns.append(jnp.concatenate(blocks, axis=0))
-        value = jnp.concatenate(columns, axis=1)
-        high, low = split(value)
-        out = dot(high, spread[...]) + dot(low, spread[...])
-        for s in range(n.phases):
-            part = out[:, s * LANES : (s + 1) * LANES]
-            field[target, s] = part.reshape(HALO, n.groups, SUB, LANES)
-
-    chunk(0, count, HALO, 0, slice(0, HALO))
-    chunk(0, count + thin, HALO, 0, slice(HALO + n.rows, 2 * HALO + n.rows))
+def spread_rows(n, pick, spread, field, target, rows):
+    columns = []
+    for t in range(n.tiles + 1):
+        blocks = [pick(t, j, g) for j in range(rows) for g in range(n.groups)]
+        columns.append(jnp.concatenate(blocks, axis=0))
+    value = jnp.concatenate(columns, axis=1)
+    high, low = split(value)
+    out = dot(high, spread[...]) + dot(low, spread[...])
+    for s in range(n.phases):
+        part = out[:, s * LANES : (s + 1) * LANES]
+        field[target, s] = part.reshape(rows, n.groups, SUB, LANES)
+
+
+def side_mask(n, place):
+    left_half = lax.broadcasted_iota(jnp.int32, (SUB, LANES), 1) < LANES // 2
+    right = jnp.where(place[1] < n.count_depth - 1, 1.0, 0.0)
+    left = jnp.where(place[1] > 0, 1.0, 0.0)
+    return jnp.where(left_half, right, left)
+
+
+def spread_own(n, place, raw, spread, field):
+    mask = side_mask(n, place)
 
     def body(i, _):
         y = pl.multiple_of(i * HALO, HALO)
-        chunk(0, 0, n.rows, y, pl.ds(y + HALO, HALO))
+
+        def pick(t, j, g):
+            value = raw[t, pl.ds(g * n.rows + y + j, SUB, stride=n.groups * n.rows), :]
+            return value * mask if t == n.tiles else value
+
+        spread_rows(n, pick, spread, field, pl.ds(y + HALO, HALO), HALO)
         return 0
 
     lax.fori_loop(0, n.rows // HALO, body, 0)
+
+
+def halo_copies(n, low, high, side_low, side_high, thin, sems):
+    count = n.planes * HALO
+    jobs = []
+    for which, (rows, side) in enumerate(((low, side_low), (high, side_high))):
+        for t in range(n.tiles):
+            cut = rows.at[0:count, t * LANES : (t + 1) * LANES]
+            jobs.append((cut, thin.at[t, which]))
+        jobs.append((side, thin.at[n.tiles, which]))
+    return [pltpu.make_async_copy(a, b, sems.at[i]) for i, (a, b) in enumerate(jobs)]
+
+
+def spread_halos(n, place, thin, spread, field):
+    mask = side_mask(n, place)
+    for which, first in ((0, 0), (1, HALO + n.rows)):
+
+        def pick(t, j, g):
+            value = thin[t, which, pl.ds(g * HALO + j, SUB, stride=n.groups * HALO), :]
+            return value * mask if t == n.tiles else value
+
+        spread_rows(n, pick, spread, field, slice(first, first + HALO), HALO)
+
+
+def edge_copies(n, low, high, thin, sems):
+    count = n.planes * HALO
+    jobs = []
+    for which, rows in enumerate((low, high)):
+        for t in range(n.tiles):
+            cut = rows.at[count : count + n.planes, t * LANES : (t + 1) * LANES]
+            jobs.append((cut, thin.at[t, which]))
+    return [pltpu.make_async_copy(a, b, sems.at[i]) for i, (a, b) in enumerate(jobs)]
+
+
+def spread_edges(n, thin, spread, image):
+    blank = jnp.zeros((SUB, LANES), F32)
+    for which, row in ((0, HALO - 1), (1, HALO + n.rows)):
+
+        def pick(t, j, g):
+            if t == n.tiles:
+                return blank
+            return thin[t, which, pl.ds(g, SUB, stride=n.groups), :]
+
+        spread_rows(n, pick, spread, image, slice(row, row + 1), 1)
 
 
 def neighbours(n, field, y0, rows):
@@ -282,17 +321,33 @@
     return low + 4 * count
 
 
-def transport(n, field, spare, speed):
-    tall = n.tall
+def stretch(n, source, target, speed, low, high, second, size):
+    done = sweep(n, source, target, speed, low, high, second)
+    if size % 4:
+        upwind_rows(n, source, target, speed, done, size % 4, second)
+
+
+def transport(n, field, spare, speed, start, stop):
+    size = stop - start
 
     def step(r, _):
-        first = 2 * r + 1
-        done = sweep(n, field, spare, speed, first, tall - first, False)
-        if (tall - 2) % 4:
-            upwind_rows(n, field, spare, speed, done, 2, False)
-        done = sweep(n, spare, field, speed, first + 1, tall - first - 1, True)
-        if tall % 4:
-            upwind_rows(n, spare, field, speed, done, 2, True)
+        k = 2 * r + 1
+        stretch(n, field, spare, speed, start + k, stop - k, False, size - 2)
+        stretch(n, spare, field, speed, start + k + 1, stop - k - 1, True, size)
+        return 0
+
+    lax.fori_loop(0, STEPS, step, 0)
+
+
+def transport_edges(n, field, spare, speed):
+    far = n.rows + HALO
+
+    def step(r, _):
+        k = 2 * r + 1
+        for k, source, target, second in ((k, field, spare, False), (k + 1, spare, field, True)):
+            for first in (k, far - k):
+                for part in range(0, HALO, 4):
+                    upwind_rows(n, source, target, speed, first + part, 4, second)
         return 0
 
     lax.fori_loop(0, STEPS, step, 0)
@@ -379,54 +434,109 @@
         packed[c * n.chunk : (c + 1) * n.chunk, :] = value
 
 
-def first_kernel(n, _, modes, bx, by, bz_e, bz_p, bx_t, by_t, spread, gather, *rest):
-    fields, rest = rest[:12], rest[12:]
-    packed, end, speed, field, spare, image, raw_a, raw_b, w, f_high, f_low, total, sems = rest
-    pulls_a = field_copies(n, *fields[:6], raw_a, sems.at[0])
-    pulls_b = field_copies(n, *fields[6:], raw_b, sems.at[1])
-    for copy in pulls_a + pulls_b:
+def table_copies(place, pairs, sems):
+    return [
+        pltpu.make_async_copy(table.at[place[axis]], held, sems.at[i])
+        for i, (table, axis, held) in enumerate(pairs)
+    ]
+
+
+def started(copies):
+    for copy in copies:
         copy.start()
-    coeffs = [-unpacked(modes[...], c, n) for c in range(3)]
-    expand_into(n, coeffs, w, bx, by.at[0], bz_e.at[0], speed)
-    for copy in pulls_a:
+    return copies
+
+
+def waited(copies):
+    for copy in copies:
         copy.wait()
-    interleave(n, raw_a, spread, field)
-    transport(n, field, spare, speed)
-    for copy in pulls_b:
-        copy.wait()
-    interleave(n, raw_b, spread, image)
-    deinterleave(n, field, gather, raw_a.at[:, : n.planes * n.rows])
-    pushes = result_copies(n, raw_a.at[:, : n.planes * n.rows], end, sems.at[2])
-    for copy in pushes:
-        copy.start()
+
+
+def own_modes(n, modes, c):
+    return jnp.concatenate([modes[c]] * n.packs, axis=1)
+
+
+def edge_rows(n, source, target, sems):
+    far = n.rows
+    spans = ((0, 2 * HALO), (far, far + 2 * HALO)) if far > HALO else ((0, n.tall),)
+    return [
+        pltpu.make_async_copy(source.at[c, p:q], target.at[c, p:q], sems.at[i, c])
+        for i, (p, q) in enumerate(spans)
+        for c in range(4)
+    ]
+
+
+def block_rows(n, sources, targets, sems):
+    own = slice(HALO, HALO + n.rows)
+    return [
+        pltpu.make_async_copy(a.at[own], b.at[own], sems.at[i])
+        for i, (a, b) in enumerate(zip(sources, targets, strict=True))
+    ]
+
+
+def inner_kernel(n, place, modes, bx, by, bz_e, spread, own_a, side_a, own_b, side_b, *rest):
+    speed_out, field_out, spare_out, image_out, *rest = rest
+    speed, field, spare, image, raw_a, raw_b, w, by_own, bz_own, sems, sems_t, sems_s, sems_f = rest
+    tables = started(table_copies(place, ((by, 0, by_own), (bz_e, 1, bz_own)), sems_t))
+    pulls_a = started(own_copies(n, own_a, side_a, raw_a, sems.at[0]))
+    pulls_b = started(own_copies(n, own_b, side_b, raw_b, sems.at[1]))
+    coeffs = [-own_modes(n, modes, c) for c in range(3)]
+    waited(tables)
+    expand_into(n, coeffs, w, bx, by_own, bz_own, speed)
+    pushes = started(edge_rows(n, speed, speed_out, sems_s))
+    waited(pulls_a)
+    spread_own(n, place, raw_a, spread, field)
+    transport(n, field, spare, speed, HALO, HALO + n.rows)
+    pushes += started(block_rows(n, (field, spare), (field_out, spare_out), sems_f))
+    waited(pulls_b)
+    spread_own(n, place, raw_b, spread, image)
+    pushes += started(block_rows(n, (image,), (image_out,), sems_f.at[2:3]))
+    waited(pushes)
+
+
+def outer_kernel(n, place, speed_in, field_in, spare_in, image_in, spread, gather, bx_t, *rest):
+    by_t, bz_p, low, high, side_low, side_high, packed, end, *rest = rest
+    speed, field, spare, image, *rest = rest
+    raw, thin, edge, f_high, f_low, total, by_own, bz_own, *rest = rest
+    sems_h, sems_e, sems_o, sems_t, sems_s, sems_f = rest
+    pulls = started(halo_copies(n, low, high, side_low, side_high, thin, sems_h))
+    speeds = started(edge_rows(n, speed_in, speed, sems_s))
+    fields = started(block_rows(n, (field_in, spare_in), (field, spare), sems_f))
+    images = started(block_rows(n, (image_in,), (image,), sems_f.at[2:3]))
+    edges = started(edge_copies(n, low, high, edge, sems_e))
+    tables = started(table_copies(place, ((by_t, 0, by_own), (bz_p, 1, bz_own)), sems_t))
+    waited(pulls)
+    spread_halos(n, place, thin, spread, field)
+    waited(speeds + fields)
+    transport_edges(n, field, spare, speed)
+    deinterleave(n, field, gather, raw)
+    pushes = started(result_copies(n, raw, end, sems_o))
+    waited(edges + images)
+    spread_edges(n, edge, spread, image)
     force(n, field, image, f_high, f_low)
-    project(n, f_high, f_low, bz_p.at[0], bx_t, by_t.at[0], total, packed)
-    for copy in pushes:
-        copy.wait()
-
-
-def second_kernel(n, _, modes, summed, factor, bx, by, bz_e, spread, gather, *rest):
-    fields, rest = rest[:6], rest[6:]
-    end, updated, speed, field, spare, raw, w, sems = rest
-    pulls = field_copies(n, *fields, raw, sems.at[0])
-    for copy in pulls:
-        copy.start()
+    waited(tables)
+    project(n, f_high, f_low, bz_own, bx_t, by_own, total, packed)
+    waited(pushes)
+
+
+def last_kernel(n, place, modes, summed, factor, bx, by, bz_e, spread, gather, *rest):
+    image, low, high, side_low, side_high, end, updated, *rest = rest
+    speed, field, spare, raw, thin, w, by_own, bz_own, sems_h, sems_o, sems_t, sems_f = rest
+    tables = started(table_copies(place, ((by, 0, by_own), (bz_e, 1, bz_own)), sems_t))
+    pulls = started(halo_copies(n, low, high, side_low, side_high, thin, sems_h))
+    images = started(block_rows(n, (image,), (field,), sems_f))
     scale = jnp.concatenate([factor[...]] * 3, axis=0)
-    packed = modes[...] + scale * summed[...]
-    coeffs = [unpacked(packed, c, n) for c in range(3)]
+    packed = scale * summed[...]
+    coeffs = [own_modes(n, modes, c) + unpacked(packed, c, n) for c in range(3)]
     for c in range(3):
         updated[c] = coeffs[c][:, : n.modes]
-    expand_into(n, coeffs, w, bx, by.at[0], bz_e.at[0], speed)
-    for copy in pulls:
-        copy.wait()
-    interleave(n, raw, spread, field)
-    transport(n, field, spare, speed)
-    deinterleave(n, field, gather, raw.at[:, : n.planes * n.rows])
-    pushes = result_copies(n, raw.at[:, : n.planes * n.rows], end, sems.at[1])
-    for copy in pushes:
-        copy.start()
-    for copy in pushes:
-        copy.wait()
+    waited(tables)
+    expand_into(n, coeffs, w, bx, by_own, bz_own, speed)
+    waited(pulls + images)
+    spread_halos(n, place, thin, spread, field)
+    transport(n, field, spare, speed, 0, n.tall)
+    deinterleave(n, field, gather, raw)
+    waited(started(result_copies(n, raw, end, sems_o)))
 
 
 def swap_with(value, axis, step):
@@ -455,28 +565,29 @@
 
 def beside(cells):
     count = lax.axis_size("dev")
-    index = lax.axis_index("dev")
-    lane = lax.broadcasted_iota(jnp.int32, (1, 1, LANES), 2)
-    head = jnp.where(lane < LANES // 2, cells[:, :, :LANES], 0.0)
-    tail = jnp.where(lane >= LANES // 2, cells[:, :, -LANES:], 0.0)
+    depth = cells.shape[-1]
     if count == 1:
-        return jnp.zeros_like(head)
+        return cells[..., :LANES]
     if count == 2:
-        return swap_with(jnp.where(index == 0, tail, head), "dev", 1)
+        start = jnp.where(lax.axis_index("dev") == 0, depth - LANES, 0)
+        return swap_with(lax.dynamic_slice_in_dim(cells, start, LANES, cells.ndim - 1), "dev", 1)
+    lane = lax.broadcasted_iota(jnp.int32, (1,) * (cells.ndim - 1) + (LANES,), cells.ndim - 1)
     ends = range(count - 1)
-    return lax.ppermute(tail, "dev", [(i, i + 1) for i in ends]) + lax.ppermute(
-        head, "dev", [(i + 1, i) for i in ends]
-    )
-
-
-def with_halos(cells):
+    from_left = lax.ppermute(cells[..., -LANES:], "dev", [(i, i + 1) for i in ends])
+    from_right = lax.ppermute(cells[..., :LANES], "dev", [(i + 1, i) for i in ends])
+    return jnp.where(lane < LANES // 2, from_right, from_left)
+
+
+def to_neighbours(last_rows, first_rows):
     ends = range(lax.axis_size("ha") - 1)
-    low = lax.ppermute(cells[:, -HALO:], "ha", [(i, i + 1) for i in ends])
-    high = lax.ppermute(cells[:, :HALO], "ha", [(i + 1, i) for i in ends])
-    side = beside(cells)
-    both = beside(jnp.concatenate([low, high], axis=1))
-    parts = (cells, low, high, side, both[:, :HALO], both[:, HALO:])
-    return [part.reshape(-1, part.shape[-1]) for part in parts]
+    low = lax.ppermute(last_rows, "ha", [(i, i + 1) for i in ends])
+    high = lax.ppermute(first_rows, "ha", [(i + 1, i) for i in ends])
+    return low, high
+
+
+def corners(low, high, count):
+    both = beside(jnp.concatenate([low[:count], high[:count]], axis=0))
+    return both[:count], both[count:]
 
 
 def per_device(brain_image, adjoint_field, velocity_modes):
@@ -492,79 +603,126 @@
     )
     t = {name: jnp.asarray(value) for name, value in n.tables().items()}
     place = jnp.stack([lax.axis_index("ha"), lax.axis_index("dev")]).astype(jnp.int32)
-    modes = velocity_modes.reshape(3, n.packs, n.chunk, n.modes).transpose(0, 2, 1, 3)
-    modes = modes.reshape(3 * n.chunk, LANES)
-    adjoint = with_halos(adjoint_field)
-    image = with_halos(brain_image)
-
-    whole = pl.BlockSpec(memory_space=pltpu.VMEM)
+    modes = velocity_modes.reshape(3, n.pairs, n.modes)
+    flat = (planes * rows, depth)
+    thin_count = planes * HALO
+
+    def rows_sent(cells):
+        return cells.reshape(-1, depth)
+
+    side_a = beside(adjoint_field).reshape(-1, LANES)
+    side_b = beside(brain_image).reshape(-1, LANES)
+    low_a, high_a = to_neighbours(
+        jnp.concatenate([rows_sent(adjoint_field[:, -HALO:]), brain_image[:, -1]], axis=0),
+        jnp.concatenate([rows_sent(adjoint_field[:, :HALO]), brain_image[:, 0]], axis=0),
+    )
+
+    held = pl.BlockSpec(memory_space=pltpu.VMEM)
+    small = pl.BlockSpec(memory_space=pltpu.SMEM)
     outside = pl.BlockSpec(memory_space=pl.ANY)
-
-    def picked(table, axis):
-        zeros = (0,) * (table.ndim - 1)
-        return pl.BlockSpec((1,) + table.shape[1:], lambda i, at: (at[axis],) + zeros)
-
     block = (n.tall, n.phases, n.groups, SUB, LANES)
-    raw = pltpu.VMEM((n.tiles + 1, planes * n.tall, LANES), F32)
-    pulls = 3 * n.tiles + 3
-    packed_shape = (3 * n.chunk, LANES)
-    flat = (planes * rows, depth)
-    params = pltpu.CompilerParams(vmem_limit_bytes=VMEM_LIMIT)
+    field_shape = jax.ShapeDtypeStruct(block, F32)
+    speed_shape = jax.ShapeDtypeStruct((4,) + block, F32)
+    raw = pltpu.VMEM((n.tiles + 1, planes * rows, LANES), F32)
+    thin = pltpu.VMEM((n.tiles + 1, 2, thin_count, LANES), F32)
+    weights = pltpu.VMEM((n.pairs, 6 * LANES), BF16)
+    semaphores = pltpu.SemaphoreType.DMA
+    by_own = pltpu.VMEM(t["by"].shape[1:], F32)
+    bz_own = pltpu.VMEM(t["bz_e"].shape[1:], BF16)
+
+    def params(mebibytes):
+        return pltpu.CompilerParams(vmem_limit_bytes=mebibytes * 2**20)
+
+    def cost(us):
+        return pl.CostEstimate(flops=int(us * 1e9), bytes_accessed=int(us * 3e6), transcendentals=0)
+
+    blocks = [pltpu.VMEM(block, F32)] * 3
+    speeds = pltpu.VMEM((4,) + block, F32)
+    speed, field, spare, image = pl.pallas_call(
+        functools.partial(inner_kernel, n),
+        in_specs=[small, held, held, outside, outside, held] + [outside] * 4,
+        out_specs=[outside] * 4,
+        out_shape=[speed_shape, field_shape, field_shape, field_shape],
+        scratch_shapes=[
+            speeds, *blocks, raw, raw, weights, by_own, bz_own,
+            semaphores((2, n.tiles + 1)), semaphores((2,)), semaphores((2, 4)), semaphores((3,)),
+        ],
+        compiler_params=params(40),
+        cost_estimate=cost(20),
+    )(
+        place, modes, t["bx"], t["by"], t["bz_e"], t["spread"], adjoint_field.reshape(flat), side_a,
+        brain_image.reshape(flat), side_b,
+    )
+
+    sent_b = (rows_sent(brain_image[:, -HALO:]), rows_sent(brain_image[:, :HALO]))
+    low_a, high_a, last_b, first_b, field = lax.optimization_barrier(
+        (low_a, high_a, *sent_b, field)
+    )
+    corner_a = corners(low_a, high_a, thin_count)
+    low_b, high_b = to_neighbours(last_b, first_b)
+
     packed, adjoint_end = pl.pallas_call(
-        functools.partial(first_kernel, n),
-        grid_spec=pltpu.PrefetchScalarGridSpec(
-            num_scalar_prefetch=1,
-            grid=(1,),
-            in_specs=[
-                whole, whole, picked(t["by"], 0), picked(t["bz_e"], 1), picked(t["bz_p"], 1),
-                whole, picked(t["by_t"], 0), whole, whole,
-            ] + [outside] * 12,
-            out_specs=[whole, outside],
-            scratch_shapes=[
-                pltpu.VMEM((4,) + block, F32),
-                pltpu.VMEM(block, F32),
-                pltpu.VMEM(block, F32),
-                pltpu.VMEM(block, F32),
-                raw,
-                raw,
-                pltpu.VMEM((n.pairs, 6 * LANES), BF16),
-                pltpu.VMEM((3, planes * rows, n.wide), BF16),
-                pltpu.VMEM((3, planes * rows, n.wide), BF16),
-                pltpu.VMEM((n.pairs, LANES), F32),
-                pltpu.SemaphoreType.DMA((3, pulls)),
-            ],
-        ),
-        out_shape=[jax.ShapeDtypeStruct(packed_shape, F32), jax.ShapeDtypeStruct(flat, F32)],
-        compiler_params=params,
+        functools.partial(outer_kernel, n),
+        in_specs=[small] + [outside] * 4 + [held] * 3 + [outside] * 6,
+        out_specs=[held, outside],
+        out_shape=[
+            jax.ShapeDtypeStruct((3 * n.chunk, LANES), F32),
+            jax.ShapeDtypeStruct(flat, F32),
+        ],
+        scratch_shapes=[
+            speeds,
+            *blocks,
+            raw,
+            thin,
+            pltpu.VMEM((n.tiles, 2, planes, LANES), F32),
+            pltpu.VMEM((3, planes * rows, n.wide), BF16),
+            pltpu.VMEM((3, planes * rows, n.wide), BF16),
+            pltpu.VMEM((n.pairs, LANES), F32),
+            pltpu.VMEM(t["by_t"].shape[1:], F32),
+            pltpu.VMEM(t["bz_p"].shape[1:], BF16),
+            semaphores((2 * n.tiles + 2,)),
+            semaphores((2 * n.tiles,)),
+            semaphores((n.tiles,)),
+            semaphores((2,)),
+            semaphores((2, 4)),
+            semaphores((3,)),
+        ],
+        compiler_params=params(44),
+        cost_estimate=cost(16),
     )(
-        place, modes, t["bx"], t["by"], t["bz_e"], t["bz_p"], t["bx_t"], t["by_t"], t["spread"],
-        t["gather"], *adjoint, *image,
-    )
+        place, speed, field, spare, image, t["spread"], t["gather"], t["bx_t"], t["by_t"], t["bz_p"],
+        low_a, high_a, *corner_a,
+    )
+    packed, low_b, high_b = lax.optimization_barrier((packed, low_b, high_b))
     summed = sum_over_devices(packed)
+    corner_b = corners(low_b, high_b, thin_count)
     image_end, updated = pl.pallas_call(
-        functools.partial(second_kernel, n),
-        grid_spec=pltpu.PrefetchScalarGridSpec(
-            num_scalar_prefetch=1,
-            grid=(1,),
-            in_specs=[
-                whole, whole, whole, whole, picked(t["by"], 0), picked(t["bz_e"], 1), whole, whole,
-            ] + [outside] * 6,
-            out_specs=[outside, whole],
-            scratch_shapes=[
-                pltpu.VMEM((4,) + block, F32),
-                pltpu.VMEM(block, F32),
-                pltpu.VMEM(block, F32),
-                raw,
-                pltpu.VMEM((n.pairs, 6 * LANES), BF16),
-                pltpu.SemaphoreType.DMA((2, pulls)),
-            ],
-        ),
+        functools.partial(last_kernel, n),
+        in_specs=[small, held, held, held, held, outside, outside, held, held] + [outside] * 5,
+        out_specs=[outside, held],
         out_shape=[
             jax.ShapeDtypeStruct(flat, F32),
             jax.ShapeDtypeStruct((3, n.pairs, n.modes), F32),
         ],
-        compiler_params=params,
-    )(place, modes, summed, t["factor"], t["bx"], t["by"], t["bz_e"], t["spread"], t["gather"], *image)
+        scratch_shapes=[
+            speeds,
+            *blocks[:2],
+            raw,
+            thin,
+            weights,
+            by_own,
+            bz_own,
+            semaphores((2 * n.tiles + 2,)),
+            semaphores((n.tiles,)),
+            semaphores((2,)),
+            semaphores((1,)),
+        ],
+        compiler_params=params(40),
+        cost_estimate=cost(28),
+    )(
+        place, modes, summed, t["factor"], t["bx"], t["by"], t["bz_e"], t["spread"], t["gather"],
+        image, low_b, high_b, *corner_b,
+    )
     return (
         adjoint_end.reshape(brain_image.shape),
         image_end.reshape(brain_image.shape),

time: 143 us -> 126 us (0.88)
  waiting for transfers between devices: 37.5 us -> 13.5 us
  local copies, waits for them, and re-layouts: 11.3 us -> 19 us
    ppermute x4, waiting for transfers between devices: 25.1 us -> 0.01 us  [the longest x2 0.01 us: to_neighbours(): low = lax.ppermute(last_rows, 'ha', [(i, i + 1) for i in ends])]
    unnamed x17 -> x42, local copies, waits for them, and re-layouts: 1.79 us -> 10.9 us
    dynamic_slice x0 -> x2, local copies, waits for them, and re-layouts: none -> 3.86 us  [beside(): lax.dynamic_slice_in_dim(cells, start, LANES, cells.ndim - 1)]
    reshape x4 -> x2, local copies, waits for them, and re-layouts: 4.52 us -> 1.01 us  [rows_sent(): return cells.reshape(-1, depth)]
    concatenate x0 -> x4, other arithmetic: none -> 2.34 us  [the longest x1 0.8 us: per_device(): jnp.concatenate([rows_sent(adjoint_field[:, :HALO]), brain_image[:, 0]],...]
    concatenate x2 -> x0, local copies, waits for them, and re-layouts: 2.04 us -> none  [with_halos(): both = beside(jnp.concatenate([low, high], axis=1))]
    slice x2 -> x5, local copies, waits for them, and re-layouts: 2.09 us -> 3.27 us  [the longest x2 2.2 us: corners(): both = beside(jnp.concatenate([low[:count], high[:count]], axis=0))]
    pallas_call x2 -> x3, Pallas kernels: 69.5 us -> 69.6 us  [the longest x1 27.4 us: per_device(): pl.pallas_call(functools.partial(last_kernel, n), in_specs=[small, held,...]
  transfers between devices with their start and end apart: 13 -> 13, of which waited for: 9 -> 5; matrix products, arithmetic and copies ran while one was open for 5% -> 5% of each run, Pallas kernels for 0% -> 34%
where the time goes in v1:
time: 126 us
  Pallas kernels  69.6 us (55%)
  starting transfers between devices  19.8 us (16%)
  local copies, waits for them, and re-layouts  19 us (15%)
  waiting for transfers between devices  13.5 us (11%)
  other arithmetic  2.5 us (2%)
    pallas_call x1, Pallas kernels, per_device(): pl.pallas_call(functools.partial(last_kernel, n), in_specs=[small, held,...  27.4 us
    pallas_call x1, Pallas kernels, per_device(): pl.pallas_call(functools.partial(inner_kernel, n), in_specs=[small, held,...  22 us
    pallas_call x1, Pallas kernels, per_device(): pl.pallas_call(functools.partial(outer_kernel, n), in_specs=[small] + [ou...  20.3 us
    ppermute x9, waiting for transfers between devices, swap_with(): return lax.ppermute(value, axis, [(i, i ^ step) for i in range(count)])  13.5 us
    unnamed x42, local copies, waits for them, and re-layouts  10.9 us
    ppermute x9, starting transfers between devices, swap_with(): return lax.ppermute(value, axis, [(i, i ^ step) for i in range(count)])  7.28 us
    ppermute x2, starting transfers between devices, to_neighbours(): high = lax.ppermute(first_rows, 'ha', [(i + 1, i) for i in ends])  6.37 us
    ppermute x2, starting transfers between devices, to_neighbours(): low = lax.ppermute(last_rows, 'ha', [(i, i + 1) for i in ends])  6.14 us
  transfers between devices with their start and end apart: 13, of which 5 were waited for; matrix products, arithmetic and copies ran while one was open for 5% of the time, Pallas kernels for 34%

profile of v1, /device:TPU:25, one launch (start us, length us, event | category | flops | bytes accessed | tf_op | source)
XLA Modules:
  0.0 125.6 jit_solution(8227880894463475897)
XLA Ops:
  0.6 0.0 copy-start.1
  0.7 2.0 %constant_dynamic-slice_fusion.1 = f32[32,32,128]{2,1,0:T(8,128)} fusion(f32[32,32,384]{2,1,0:T(8,128)} %param.13, s32[]{:T(128)S(6)} %select_n.30), kind=kLoop, calls=%fused_computation.20 | loop fusion | bytes 1048580 | tf_op jit(solution)/shard_map/dynamic_slice | solution.py:573
  2.6 0.7 collective-permute-start
  3.3 1.9 %constant_dynamic-slice_fusion = f32[32,32,128]{2,1,0:T(8,128)} fusion(f32[32,32,384]{2,1,0:T(8,128)} %param.12, s32[]{:T(128)S(6)} %select_n.30), kind=kLoop, calls=%fused_computation.19 | loop fusion | bytes 1048580 | tf_op jit(solution)/shard_map/dynamic_slice | solution.py:573
  5.2 0.1 collective-permute-start.1
  5.3 0.0 copy-done.1
  5.3 0.1 slice_bitcast_fusion.2
  5.4 0.0 copy-done
  5.4 0.1 fusion.2
  5.5 0.0 copy-start.11
  5.5 0.0 copy-start.13
  5.5 0.8 pad_maximum_fusion
  6.3 3.1 %collective-permute-start.2 = (f32[288,384]{1,0:T(8,128)}, f32[288,384]{1,0:T(8,128)}, u32[]{:S(2)}, u32[]{:S(2)}) collective-permute-start(f32[288,384]{1,0:T(8,128)} %pad_maximum_fusion), channel_id=1, source_target_pairs={{0,2},{2,4},{4,6},{6,8},{8,10},{10,12},{12,14},{1,3},{3,5},{5,7},{... | collective-permute-start | bytes 1327112 | tf_op jit(solution)/shard_map/ppermute | solution.py:583
  9.4 0.8 pad_maximum_fusion.1
  10.2 3.0 %collective-permute-start.3 = (f32[288,384]{1,0:T(8,128)}, f32[288,384]{1,0:T(8,128)}, u32[]{:S(2)}, u32[]{:S(2)}) collective-permute-start(f32[288,384]{1,0:T(8,128)} %pad_maximum_fusion.1), channel_id=1, source_target_pairs={{2,0},{4,2},{6,4},{8,6},{10,8},{12,10},{14,12},{3,1},{5,3},{7,5},{... | collective-permute-start | bytes 1327112 | tf_op jit(solution)/shard_map/ppermute | solution.py:584
  13.3 0.0 copy-start.2
  13.3 0.0 copy-start.6
  13.3 0.1 pad_add_fusion.place
  13.4 1.0 slice_bitcast_fusion
  14.3 0.0 collective-permute-done
  14.3 0.0 collective-permute-done.1
  14.4 0.2 copy-done.2
  14.6 0.4 copy-done.6
  14.9 1.0 copy-done.8
  16.0 22.0 %shard_map.139 = (f32[4,48,4,4,8,128]{5,4,3,2,1,0:T(8,128)}, f32[48,4,4,8,128]{4,3,2,1,0:T(8,128)S(1)}, f32[48,4,4,8,128]{4,3,2,1,0:T(8,128)S(1)}, f32[48,4,4,8,128]{4,3,2,1,0:T(8,128)}) custom-call(s32[2]{0:T(128)S(1)} %pad_add_fusion.place, f32[3,512,32]{2,1,0:T(8,128)S(1)} %bitcast.33, f32[32,512]{1,0:T(8,128)S(1)} %copy-done.13, ...), custom_call_target="tpu_custom_call" | custom-call | flops 20000000000 | bytes 60000000 | tf_op jit(solution)/shard_map/pallas_call | solution.py:641
  38.0 1.7 %copy-done.17 = f32[48,4,4,8,128]{4,3,2,1,0:T(8,128)} copy-done((f32[48,4,4,8,128]{4,3,2,1,0:T(8,128)}, f32[48,4,4,8,128]{4,3,2,1,0:T(8,128)S(1)}, u32[]{:S(2)}) %copy-start.17) | copy-done | bytes 3145752
  39.7 1.7 %copy-done.19 = f32[48,4,4,8,128]{4,3,2,1,0:T(8,128)} copy-done((f32[48,4,4,8,128]{4,3,2,1,0:T(8,128)}, f32[48,4,4,8,128]{4,3,2,1,0:T(8,128)S(1)}, u32[]{:S(2)}) %copy-start.19) | copy-done | bytes 3145752
  41.3 0.0 collective-permute-done.2.rest_2_
  41.3 0.0 collective-permute-done.3.rest_3_
  41.3 0.0 copy-start.9
  41.3 0.0 copy-start.10
  41.4 1.2 slice.42
  42.5 1.0 slice.43
  43.6 0.7 fusion.1
  44.3 0.9 collective-permute-start.4
  45.2 3.0 %collective-permute-start.5 = (f32[256,384]{1,0:T(8,128)}, f32[256,384]{1,0:T(8,128)S(1)}, u32[]{:S(2)}, u32[]{:S(2)}) collective-permute-start(f32[256,384]{1,0:T(8,128)} %get-tuple-element.28), channel_id=1, source_target_pairs={{0,2},{2,4},{4,6},{6,8},{8,10},{10,12},{12,14},{1,3},{3,5},{5,7},{... | collective-permute-start | bytes 1179656 | tf_op jit(solution)/shard_map/ppermute | solution.py:583
  48.2 3.3 %collective-permute-start.6 = (f32[256,384]{1,0:T(8,128)}, f32[256,384]{1,0:T(8,128)S(1)}, u32[]{:S(2)}, u32[]{:S(2)}) collective-permute-start(f32[256,384]{1,0:T(8,128)} %get-tuple-element.29), channel_id=1, source_target_pairs={{2,0},{4,2},{6,4},{8,6},{10,8},{12,10},{14,12},{3,1},{5,3},{7,5},{... | collective-permute-start | bytes 1179656 | tf_op jit(solution)/shard_map/ppermute | solution.py:584
  51.6 0.0 collective-permute-done.4
  51.6 1.0 fusion.4
  52.6 0.0 copy-start.5
  52.6 1.2 copy-done.5
  53.9 0.8 copy-done.15
  54.7 1.9 %copy-done.18 = f32[48,4,4,8,128]{4,3,2,1,0:T(8,128)S(1)} copy-done((f32[48,4,4,8,128]{4,3,2,1,0:T(8,128)S(1)}, f32[48,4,4,8,128]{4,3,2,1,0:T(8,128)}, u32[]{:S(2)}) %copy-start.18) | copy-done | bytes 3145752
  56.6 20.3 %shard_map.140 = (f32[384,128]{1,0:T(8,128)S(1)}, f32[1024,384]{1,0:T(8,128)}) custom-call(s32[2]{0:T(128)S(1)} %pad_add_fusion.place, f32[4,48,4,4,8,128]{5,4,3,2,1,0:T(8,128)} %get-tuple-element.19.speed_in, f32[48,4,4,8,128]{4,3,2,1,0:T(8,128)S(1)} %copy-done.18, f32[48,4,4,8,128]{4,3,2,1,0:T(8,128)} %copy-done.19, ...), custom_call_target="tpu_custom_call" | custom-call | flops 16000000000 | bytes 48000000 | tf_op jit(solution)/shard_map/pallas_call | solution.py:664
  76.9 0.0 collective-permute-done.5.rest_1_
  76.9 0.0 collective-permute-done.6.rest_2_
  76.9 0.7 collective-permute-start.7
  77.6 0.9 collective-permute-done.7
  78.5 0.0 copy-start.3
  78.6 0.0 copy-start.7
  78.6 0.0 copy-start.12
  78.6 0.0 copy-start.14
  78.6 0.3 collective-permute-start.8
  78.9 0.7 collective-permute-start.12
  79.6 3.1 %collective-permute-done.8 = f32[192,128]{1,0:T(8,128)S(1)} collective-permute-done((f32[192,128]{1,0:T(8,128)S(1)}, f32[192,128]{1,0:T(8,128)S(1)}, u32[]{:S(2)}, u32[]{:S(2)}) %collective-permute-start.8) | collective-permute-done | bytes 98336 | tf_op jit(solution)/shard_map/ppermute | solution.py:544
  82.7 0.2 collective-permute-start.9
  82.9 3.3 %collective-permute-done.9 = f32[192,128]{1,0:T(8,128)S(1)} collective-permute-done((f32[192,128]{1,0:T(8,128)S(1)}, f32[192,128]{1,0:T(8,128)S(1)}, u32[]{:S(2)}, u32[]{:S(2)}) %collective-permute-start.9) | collective-permute-done | bytes 98336 | tf_op jit(solution)/shard_map/ppermute | solution.py:544
  86.2 0.1 collective-permute-start.10
  86.3 5.3 %collective-permute-done.10 = f32[192,128]{1,0:T(8,128)S(1)} collective-permute-done((f32[192,128]{1,0:T(8,128)S(1)}, f32[192,128]{1,0:T(8,128)S(1)}, u32[]{:S(2)}, u32[]{:S(2)}) %collective-permute-start.10) | collective-permute-done | bytes 98336 | tf_op jit(solution)/shard_map/ppermute | solution.py:544
  91.6 3.5 %collective-permute-start.11 = (f32[192,128]{1,0:T(8,128)S(1)}, f32[192,128]{1,0:T(8,128)S(1)}, u32[]{:S(2)}, u32[]{:S(2)}) collective-permute-start(f32[192,128]{1,0:T(8,128)S(1)} %add.29), channel_id=1, source_target_pairs={{0,1},{1,0},{2,3},{3,2},{4,5},{5,4},{6,7},{7,6},{8,9},{9,8},{10,11... | collective-permute-start | bytes 294920 | tf_op jit(solution)/shard_map/ppermute | solution.py:544
  95.2 0.0 collective-permute-done.12
  95.2 0.9 collective-permute-done.11
  96.2 1.9 %copy-done.16 = f32[48,4,4,8,128]{4,3,2,1,0:T(8,128)S(1)} copy-done((f32[48,4,4,8,128]{4,3,2,1,0:T(8,128)S(1)}, f32[48,4,4,8,128]{4,3,2,1,0:T(8,128)}, u32[]{:S(2)}) %copy-start.16) | copy-done | bytes 3145752
  98.1 27.4 %shard_map.141 = (f32[1024,384]{1,0:T(8,128)}, f32[3,512,32]{2,1,0:T(8,128)}) custom-call(s32[2]{0:T(128)S(1)} %pad_add_fusion.place, f32[3,512,32]{2,1,0:T(8,128)S(1)} %bitcast.34, f32[384,128]{1,0:T(8,128)S(1)} %pad_maximum_fusion.2.summed, f32[128,128]{1,0:T(8,128)S(1)} %copy-done.14, f32[32,512]{1,0:T(8,128)S(1)} %copy-done.13, ...), custom_call_target="tpu_custom_call" | custom-call | flops 28000000000 | bytes 84000000 | tf_op jit(solution)/shard_map/pallas_call | solution.py:699
  (28 shorter events, 0.2 us)
Async XLA Ops:
  0.6 4.7 %copy-start.1 = (f32[32,32,384]{2,1,0:T(8,128)S(1)}, f32[32,32,384]{2,1,0:T(8,128)}, u32[]{:S(2)}) copy-start(f32[32,32,384]{2,1,0:T(8,128)} %param.13) | copy-start | bytes 4718596
  2.6 2.7 %copy-start = (f32[32,32,384]{2,1,0:T(8,128)S(1)}, f32[32,32,384]{2,1,0:T(8,128)}, u32[]{:S(2)}) copy-start(f32[32,32,384]{2,1,0:T(8,128)} %param.12) | copy-start | bytes 4718596
  2.6 11.7 %collective-permute-start = (f32[32,32,128]{2,1,0:T(8,128)}, f32[32,32,128]{2,1,0:T(8,128)}, u32[]{:S(2)}, u32[]{:S(2)}) collective-permute-start(f32[32,32,128]{2,1,0:T(8,128)} %constant_dynamic-slice_fusion.1), channel_id=1, source_target_pairs={{0,1},{1,0},{2,3},{3,2},{4,5},{5,4},{6,7},{7,6},{8,9},{9,8},{10,11... | collective-permute-start | bytes 1572872 | tf_op jit(solution)/shard_map/ppermute | solution.py:544
  5.2 9.2 %collective-permute-start.1 = (f32[32,32,128]{2,1,0:T(8,128)}, f32[32,32,128]{2,1,0:T(8,128)}, u32[]{:S(2)}, u32[]{:S(2)}) collective-permute-start(f32[32,32,128]{2,1,0:T(8,128)} %constant_dynamic-slice_fusion), channel_id=1, source_target_pairs={{0,1},{1,0},{2,3},{3,2},{4,5},{5,4},{6,7},{7,6},{8,9},{9,8},{10,11... | collective-permute-start | bytes 1572872 | tf_op jit(solution)/shard_map/ppermute | solution.py:544
  5.5 8.9 %copy-start.11 = (bf16[2,128,512]{2,1,0:T(8,128)(2,1)S(1)}, bf16[2,128,512]{2,1,0:T(8,128)(2,1)}, u32[]{:S(2)}) copy-start(bf16[2,128,512]{2,1,0:T(8,128)(2,1)} %constant.47.clone.bz_e) | copy-start | bytes 786436
  5.5 8.9 %copy-start.13 = (f32[32,512]{1,0:T(8,128)S(1)}, f32[32,512]{1,0:T(8,128)}, u32[]{:S(2)}) copy-start(f32[32,512]{1,0:T(8,128)} %constant.43.clone.bx) | copy-start | bytes 196612
  6.3 35.0 %collective-permute-start.2 = (f32[288,384]{1,0:T(8,128)}, f32[288,384]{1,0:T(8,128)}, u32[]{:S(2)}, u32[]{:S(2)}) collective-permute-start(f32[288,384]{1,0:T(8,128)} %pad_maximum_fusion), channel_id=1, source_target_pairs={{0,2},{2,4},{4,6},{6,8},{8,10},{10,12},{12,14},{1,3},{3,5},{5,7},{... | collective-permute-start | bytes 1327112 | tf_op jit(solution)/shard_map/ppermute | solution.py:583
  10.2 31.1 %collective-permute-start.3 = (f32[288,384]{1,0:T(8,128)}, f32[288,384]{1,0:T(8,128)}, u32[]{:S(2)}, u32[]{:S(2)}) collective-permute-start(f32[288,384]{1,0:T(8,128)} %pad_maximum_fusion.1), channel_id=1, source_target_pairs={{2,0},{4,2},{6,4},{8,6},{10,8},{12,10},{14,12},{3,1},{5,3},{7,5},{... | collective-permute-start | bytes 1327112 | tf_op jit(solution)/shard_map/ppermute | solution.py:584
  13.3 1.3 %copy-start.2 = (f32[3,16,32,32]{3,2,1,0:T(8,128)S(1)}, f32[3,16,32,32]{3,2,1,0:T(8,128)}, u32[]{:S(2)}) copy-start(f32[3,16,32,32]{3,2,1,0:T(8,128)} %param.14) | copy-start | bytes 589828
  13.3 1.6 %copy-start.6 = (f32[8,48,512]{2,1,0:T(8,128)S(1)}, f32[8,48,512]{2,1,0:T(8,128)}, u32[]{:S(2)}) copy-start(f32[8,48,512]{2,1,0:T(8,128)} %constant.44.clone.by) | copy-start | bytes 2359300
  14.9 1.0 copy-start.8
  38.0 1.7 %copy-start.17 = (f32[48,4,4,8,128]{4,3,2,1,0:T(8,128)}, f32[48,4,4,8,128]{4,3,2,1,0:T(8,128)S(1)}, u32[]{:S(2)}) copy-start(f32[48,4,4,8,128]{4,3,2,1,0:T(8,128)S(1)} %get-tuple-element.21.field_in) | copy-start | bytes 9437188
  39.7 1.7 %copy-start.19 = (f32[48,4,4,8,128]{4,3,2,1,0:T(8,128)}, f32[48,4,4,8,128]{4,3,2,1,0:T(8,128)S(1)}, u32[]{:S(2)}) copy-start(f32[48,4,4,8,128]{4,3,2,1,0:T(8,128)S(1)} %get-tuple-element.22.spare_in) | copy-start | bytes 9437188
  41.3 11.3 %copy-start.4 = (bf16[2,3,512,256]{3,2,1,0:T(8,128)(2,1)S(1)}, bf16[2,3,512,256]{3,2,1,0:T(8,128)(2,1)}, u32[]{:S(2)}) copy-start(bf16[2,3,512,256]{3,2,1,0:T(8,128)(2,1)} %constant.48.clone.rest_1_) | copy-start | bytes 4718596
  41.3 11.3 %copy-start.9 = (bf16[512,512]{1,0:T(8,128)(2,1)S(1)}, bf16[512,512]{1,0:T(8,128)(2,1)}, u32[]{:S(2)}) copy-start(bf16[512,512]{1,0:T(8,128)(2,1)} %constant.49.clone.spread) | copy-start | bytes 1572868
  41.3 11.3 %copy-start.10 = (bf16[512,384]{1,0:T(8,128)(2,1)S(1)}, bf16[512,384]{1,0:T(8,128)(2,1)}, u32[]{:S(2)}) copy-start(bf16[512,384]{1,0:T(8,128)(2,1)} %constant.50.clone.gather) | copy-start | bytes 1179652
  44.3 7.3 %collective-permute-start.4 = (f32[512,128]{1,0:T(8,128)}, f32[512,128]{1,0:T(8,128)}, u32[]{:S(2)}, u32[]{:S(2)}) collective-permute-start(f32[512,128]{1,0:T(8,128)} %fusion.1), channel_id=1, source_target_pairs={{0,1},{1,0},{2,3},{3,2},{4,5},{5,4},{6,7},{7,6},{8,9},{9,8},{10,11... | collective-permute-start | bytes 786440 | tf_op jit(solution)/shard_map/ppermute | solution.py:544
  45.2 31.6 %collective-permute-start.5 = (f32[256,384]{1,0:T(8,128)}, f32[256,384]{1,0:T(8,128)S(1)}, u32[]{:S(2)}, u32[]{:S(2)}) collective-permute-start(f32[256,384]{1,0:T(8,128)} %get-tuple-element.28), channel_id=1, source_target_pairs={{0,2},{2,4},{4,6},{6,8},{8,10},{10,12},{12,14},{1,3},{3,5},{5,7},{... | collective-permute-start | bytes 1179656 | tf_op jit(solution)/shard_map/ppermute | solution.py:583
  48.2 28.6 %collective-permute-start.6 = (f32[256,384]{1,0:T(8,128)}, f32[256,384]{1,0:T(8,128)S(1)}, u32[]{:S(2)}, u32[]{:S(2)}) collective-permute-start(f32[256,384]{1,0:T(8,128)} %get-tuple-element.29), channel_id=1, source_target_pairs={{2,0},{4,2},{6,4},{8,6},{10,8},{12,10},{14,12},{3,1},{5,3},{7,5},{... | collective-permute-start | bytes 1179656 | tf_op jit(solution)/shard_map/ppermute | solution.py:584
  52.6 1.2 copy-start.5
  53.9 0.8 copy-start.15
  54.7 1.9 %copy-start.18 = (f32[48,4,4,8,128]{4,3,2,1,0:T(8,128)S(1)}, f32[48,4,4,8,128]{4,3,2,1,0:T(8,128)}, u32[]{:S(2)}) copy-start(f32[48,4,4,8,128]{4,3,2,1,0:T(8,128)} %copy-done.17) | copy-start | bytes 9437188
  76.9 1.6 %collective-permute-start.7 = (f32[192,128]{1,0:T(8,128)S(1)}, f32[192,128]{1,0:T(8,128)S(1)}, u32[]{:S(2)}, u32[]{:S(2)}) collective-permute-start(f32[192,128]{1,0:T(8,128)S(1)} %dynamic-slice_bitcast_fusion), channel_id=1, source_target_pairs={{0,1},{1,0},{2,3},{3,2},{4,5},{5,4},{6,7},{7,6},{8,9},{9,8},{10,11... | collective-permute-start | bytes 294920 | tf_op jit(solution)/shard_map/ppermute | solution.py:544
  78.5 17.6 %copy-start.3 = (f32[3,16,32,32]{3,2,1,0:T(8,128)S(1)}, f32[3,16,32,32]{3,2,1,0:T(8,128)}, u32[]{:S(2)}) copy-start(f32[3,16,32,32]{3,2,1,0:T(8,128)} %param.14) | copy-start | bytes 589828
  78.6 17.6 %copy-start.7 = (f32[8,48,512]{2,1,0:T(8,128)S(1)}, f32[8,48,512]{2,1,0:T(8,128)}, u32[]{:S(2)}) copy-start(f32[8,48,512]{2,1,0:T(8,128)} %constant.44.clone.by) | copy-start | bytes 2359300
  78.6 17.6 %copy-start.12 = (bf16[2,128,512]{2,1,0:T(8,128)(2,1)S(1)}, bf16[2,128,512]{2,1,0:T(8,128)(2,1)}, u32[]{:S(2)}) copy-start(bf16[2,128,512]{2,1,0:T(8,128)(2,1)} %constant.47.clone.bz_e) | copy-start | bytes 786436
  78.6 17.6 %copy-start.14 = (f32[128,128]{1,0:T(8,128)S(1)}, f32[128,128]{1,0:T(8,128)}, u32[]{:S(2)}) copy-start(f32[128,128]{1,0:T(8,128)} %constant.51.clone.factor) | copy-start | bytes 196612
  78.6 4.1 %collective-permute-start.8 = (f32[192,128]{1,0:T(8,128)S(1)}, f32[192,128]{1,0:T(8,128)S(1)}, u32[]{:S(2)}, u32[]{:S(2)}) collective-permute-start(f32[192,128]{1,0:T(8,128)S(1)} %bitcast_add_fusion), channel_id=1, source_target_pairs={{0,2},{2,0},{4,6},{6,4},{8,10},{10,8},{12,14},{14,12},{1,3},{3,1},... | collective-permute-start | bytes 294920 | tf_op jit(solution)/shard_map/ppermute | solution.py:544
  78.9 16.3 %collective-permute-start.12 = (f32[512,128]{1,0:T(8,128)S(1)}, f32[512,128]{1,0:T(8,128)S(1)}, u32[]{:S(2)}, u32[]{:S(2)}) collective-permute-start(f32[512,128]{1,0:T(8,128)S(1)} %fusion), channel_id=1, source_target_pairs={{0,1},{1,0},{2,3},{3,2},{4,5},{5,4},{6,7},{7,6},{8,9},{9,8},{10,11... | collective-permute-start | bytes 786440 | tf_op jit(solution)/shard_map/ppermute | solution.py:544
  82.7 3.5 %collective-permute-start.9 = (f32[192,128]{1,0:T(8,128)S(1)}, f32[192,128]{1,0:T(8,128)S(1)}, u32[]{:S(2)}, u32[]{:S(2)}) collective-permute-start(f32[192,128]{1,0:T(8,128)S(1)} %add.27), channel_id=1, source_target_pairs={{0,4},{2,6},{4,0},{6,2},{8,12},{10,14},{12,8},{14,10},{1,5},{3,7},... | collective-permute-start | bytes 294920 | tf_op jit(solution)/shard_map/ppermute | solution.py:544
  86.2 5.4 %collective-permute-start.10 = (f32[192,128]{1,0:T(8,128)S(1)}, f32[192,128]{1,0:T(8,128)S(1)}, u32[]{:S(2)}, u32[]{:S(2)}) collective-permute-start(f32[192,128]{1,0:T(8,128)S(1)} %add.28), channel_id=1, source_target_pairs={{0,8},{2,10},{4,12},{6,14},{8,0},{10,2},{12,4},{14,6},{1,9},{3,11}... | collective-permute-start | bytes 294920 | tf_op jit(solution)/shard_map/ppermute | solution.py:544
  91.6 4.5 %collective-permute-start.11 = (f32[192,128]{1,0:T(8,128)S(1)}, f32[192,128]{1,0:T(8,128)S(1)}, u32[]{:S(2)}, u32[]{:S(2)}) collective-permute-start(f32[192,128]{1,0:T(8,128)S(1)} %add.29), channel_id=1, source_target_pairs={{0,1},{1,0},{2,3},{3,2},{4,5},{5,4},{6,7},{7,6},{8,9},{9,8},{10,11... | collective-permute-start | bytes 294920 | tf_op jit(solution)/shard_map/ppermute | solution.py:544
  96.2 1.9 %copy-start.16 = (f32[48,4,4,8,128]{4,3,2,1,0:T(8,128)S(1)}, f32[48,4,4,8,128]{4,3,2,1,0:T(8,128)}, u32[]{:S(2)}) copy-start(f32[48,4,4,8,128]{4,3,2,1,0:T(8,128)} %get-tuple-element.23.image_in.rest_0_) | copy-start | bytes 9437188

commit v2 on v1

--- a/solution.py
+++ b/solution.py
@@ -647,7 +647,7 @@
             speeds, *blocks, raw, raw, weights, by_own, bz_own,
             semaphores((2, n.tiles + 1)), semaphores((2,)), semaphores((2, 4)), semaphores((3,)),
         ],
-        compiler_params=params(40),
+        compiler_params=params(60),
         cost_estimate=cost(20),
     )(
         place, modes, t["bx"], t["by"], t["bz_e"], t["spread"], adjoint_field.reshape(flat), side_a,
@@ -687,7 +687,7 @@
             semaphores((2, 4)),
             semaphores((3,)),
         ],
-        compiler_params=params(44),
+        compiler_params=params(60),
         cost_estimate=cost(16),
     )(
         place, speed, field, spare, image, t["spread"], t["gather"], t["bx_t"], t["by_t"], t["bz_p"],
@@ -717,7 +717,7 @@
             semaphores((2,)),
             semaphores((1,)),
         ],
-        compiler_params=params(40),
+        compiler_params=params(60),
         cost_estimate=cost(28),
     )(
         place, modes, summed, t["factor"], t["bx"], t["by"], t["bz_e"], t["spread"], t["gather"],

time: 126 us -> 121 us (0.960)
  local copies, waits for them, and re-layouts: 19 us -> 8.54 us
  Pallas kernels: 69.6 us -> 75.4 us
    unnamed x42 -> x10, local copies, waits for them, and re-layouts: 10.9 us -> 0.03 us
    pallas_call x1, Pallas kernels: 20.3 us -> 22.7 us  [per_device(): pl.pallas_call(functools.partial(outer_kernel, n), in_specs=[small] + [ou...]
    pallas_call x1, Pallas kernels: 22 us -> 24 us  [per_device(): pl.pallas_call(functools.partial(inner_kernel, n), in_specs=[small, held,...]
    pallas_call x1, Pallas kernels: 27.4 us -> 28.7 us  [per_device(): pl.pallas_call(functools.partial(last_kernel, n), in_specs=[small, held,...]
  transfers between devices with their start and end apart: 13 -> 13, of which waited for: 5 -> 5; matrix products, arithmetic and copies ran while one was open for 5% -> 4% of each run, Pallas kernels for 34% -> 39%
where the time goes in v2:
time: 121 us; the launch traced here: 120 us
  Pallas kernels  75.4 us (62%)
  starting transfers between devices  19.8 us (16%)
  waiting for transfers between devices  12.8 us (11%)
  local copies, waits for them, and re-layouts  8.54 us (7%)
  other arithmetic  2.4 us (2%)
    pallas_call x1, Pallas kernels, per_device(): pl.pallas_call(functools.partial(last_kernel, n), in_specs=[small, held,...  28.7 us
    pallas_call x1, Pallas kernels, per_device(): pl.pallas_call(functools.partial(inner_kernel, n), in_specs=[small, held,...  24 us
    pallas_call x1, Pallas kernels, per_device(): pl.pallas_call(functools.partial(outer_kernel, n), in_specs=[small] + [ou...  22.7 us
    ppermute x9, waiting for transfers between devices, swap_with(): return lax.ppermute(value, axis, [(i, i ^ step) for i in range(count)])  12.8 us
    ppermute x9, starting transfers between devices, swap_with(): return lax.ppermute(value, axis, [(i, i ^ step) for i in range(count)])  7.28 us
    ppermute x2, starting transfers between devices, to_neighbours(): high = lax.ppermute(first_rows, 'ha', [(i + 1, i) for i in ends])  6.39 us
    ppermute x2, starting transfers between devices, to_neighbours(): low = lax.ppermute(last_rows, 'ha', [(i, i + 1) for i in ends])  6.14 us
    dynamic_slice x2, local copies, waits for them, and re-layouts, beside(): lax.dynamic_slice_in_dim(cells, start, LANES, cells.ndim - 1)  3.86 us
  transfers between devices with their start and end apart: 13, of which 5 were waited for; matrix products, arithmetic and copies ran while one was open for 4% of the time, Pallas kernels for 39%

profile of v2, /device:TPU:25, one launch (start us, length us, event | category | flops | bytes accessed | tf_op | source)
XLA Modules:
  0.0 120.0 jit_solution(14230493276962663214)
XLA Ops:
  0.6 0.0 copy-start.1
  0.7 2.0 %constant_dynamic-slice_fusion.1 = f32[32,32,128]{2,1,0:T(8,128)} fusion(f32[32,32,384]{2,1,0:T(8,128)} %param.13, s32[]{:T(128)S(6)} %select_n.30), kind=kLoop, calls=%fused_computation.20 | loop fusion | bytes 1048580 | tf_op jit(solution)/shard_map/dynamic_slice | solution.py:573
  2.6 0.0 copy-start
  2.6 0.7 collective-permute-start
  3.3 1.9 %constant_dynamic-slice_fusion = f32[32,32,128]{2,1,0:T(8,128)} fusion(f32[32,32,384]{2,1,0:T(8,128)} %param.12, s32[]{:T(128)S(6)} %select_n.30), kind=kLoop, calls=%fused_computation.19 | loop fusion | bytes 1048580 | tf_op jit(solution)/shard_map/dynamic_slice | solution.py:573
  5.2 0.1 collective-permute-start.1
  5.3 0.0 copy-done.1
  5.3 0.1 slice_bitcast_fusion.2
  5.4 0.0 copy-done
  5.4 0.1 fusion.2
  5.5 3.1 %collective-permute-start.2 = (f32[288,384]{1,0:T(8,128)S(1)}, f32[288,384]{1,0:T(8,128)}, u32[]{:S(2)}, u32[]{:S(2)}) collective-permute-start(f32[288,384]{1,0:T(8,128)S(1)} %pad_maximum_fusion), channel_id=1, source_target_pairs={{0,2},{2,4},{4,6},{6,8},{8,10},{10,12},{12,14},{1,3},{3,5},{5,7},{... | collective-permute-start | bytes 1327112 | tf_op jit(solution)/shard_map/ppermute | solution.py:583
  8.7 3.0 %collective-permute-start.3 = (f32[288,384]{1,0:T(8,128)S(1)}, f32[288,384]{1,0:T(8,128)}, u32[]{:S(2)}, u32[]{:S(2)}) collective-permute-start(f32[288,384]{1,0:T(8,128)S(1)} %pad_maximum_fusion.1), channel_id=1, source_target_pairs={{2,0},{4,2},{6,4},{8,6},{10,8},{12,10},{14,12},{3,1},{5,3},{7,5},{... | collective-permute-start | bytes 1327112 | tf_op jit(solution)/shard_map/ppermute | solution.py:584
  11.8 0.7 pad_add_fusion.place
  12.4 0.1 slice_bitcast_fusion
  12.5 0.0 collective-permute-done
  12.5 0.0 collective-permute-done.1
  12.5 24.0 %shard_map.139 = (f32[4,48,4,4,8,128]{5,4,3,2,1,0:T(8,128)}, f32[48,4,4,8,128]{4,3,2,1,0:T(8,128)}, f32[48,4,4,8,128]{4,3,2,1,0:T(8,128)}, f32[48,4,4,8,128]{4,3,2,1,0:T(8,128)}) custom-call(s32[2]{0:T(128)} %pad_add_fusion.place, f32[3,512,32]{2,1,0:T(8,128)} %bitcast.35, f32[32,512]{1,0:T(8,128)} %constant.43.clone.bx, f32[8,48,512]{2,1,0:T(8,128)} %constant.44.clone.by, ...), custom_call_target="tpu_custom_call" | custom-call | flops 20000000000 | bytes 60000000 | tf_op jit(solution)/shard_map/pallas_call | solution.py:641
  36.5 0.0 collective-permute-done.2.rest_2_
  36.5 0.0 collective-permute-done.3.rest_3_
  36.5 1.0 slice.42
  37.5 1.0 slice.43
  38.6 1.0 collective-permute-start.4
  39.6 3.0 %collective-permute-start.5 = (f32[256,384]{1,0:T(8,128)S(1)}, f32[256,384]{1,0:T(8,128)S(1)}, u32[]{:S(2)}, u32[]{:S(2)}) collective-permute-start(f32[256,384]{1,0:T(8,128)S(1)} %get-tuple-element.28), channel_id=1, source_target_pairs={{0,2},{2,4},{4,6},{6,8},{8,10},{10,12},{12,14},{1,3},{3,5},{5,7},{... | collective-permute-start | bytes 1179656 | tf_op jit(solution)/shard_map/ppermute | solution.py:583
  42.6 3.4 %collective-permute-start.6 = (f32[256,384]{1,0:T(8,128)S(1)}, f32[256,384]{1,0:T(8,128)S(1)}, u32[]{:S(2)}, u32[]{:S(2)}) collective-permute-start(f32[256,384]{1,0:T(8,128)S(1)} %get-tuple-element.29), channel_id=1, source_target_pairs={{2,0},{4,2},{6,4},{8,6},{10,8},{12,10},{14,12},{3,1},{5,3},{7,5},{... | collective-permute-start | bytes 1179656 | tf_op jit(solution)/shard_map/ppermute | solution.py:584
  46.0 0.0 collective-permute-done.4
  46.0 0.7 fusion.4
  46.7 22.7 %shard_map.140 = (f32[384,128]{1,0:T(8,128)}, f32[1024,384]{1,0:T(8,128)}) custom-call(s32[2]{0:T(128)} %pad_add_fusion.place, f32[4,48,4,4,8,128]{5,4,3,2,1,0:T(8,128)} %get-tuple-element.19.speed_in, f32[48,4,4,8,128]{4,3,2,1,0:T(8,128)} %get-tuple-element.21.field_in, f32[48,4,4,8,128]{4,3,2,1,0:T(8,128)} %get-tuple-element.22.spare_in, ...), custom_call_target="tpu_custom_call" | custom-call | flops 16000000000 | bytes 48000000 | tf_op jit(solution)/shard_map/pallas_call | solution.py:664
  69.4 0.0 collective-permute-done.5.rest_1_
  69.4 0.0 copy-start.2
  69.4 0.0 collective-permute-done.6.rest_2_
  69.4 0.0 copy-start.3
  69.5 1.0 dynamic-slice_bitcast_fusion
  70.5 0.6 collective-permute-start.7
  71.0 0.9 collective-permute-done.7
  72.0 0.9 bitcast_add_fusion
  72.9 0.3 collective-permute-start.8
  73.2 0.7 collective-permute-start.12
  73.9 3.1 %collective-permute-done.8 = f32[192,128]{1,0:T(8,128)S(1)} collective-permute-done((f32[192,128]{1,0:T(8,128)S(1)}, f32[192,128]{1,0:T(8,128)S(1)}, u32[]{:S(2)}, u32[]{:S(2)}) %collective-permute-start.8) | collective-permute-done | bytes 98336 | tf_op jit(solution)/shard_map/ppermute | solution.py:544
  77.0 0.2 collective-permute-start.9
  77.2 3.3 %collective-permute-done.9 = f32[192,128]{1,0:T(8,128)S(1)} collective-permute-done((f32[192,128]{1,0:T(8,128)S(1)}, f32[192,128]{1,0:T(8,128)S(1)}, u32[]{:S(2)}, u32[]{:S(2)}) %collective-permute-start.9) | collective-permute-done | bytes 98336 | tf_op jit(solution)/shard_map/ppermute | solution.py:544
  80.5 0.1 collective-permute-start.10
  80.7 5.3 %collective-permute-done.10 = f32[192,128]{1,0:T(8,128)S(1)} collective-permute-done((f32[192,128]{1,0:T(8,128)S(1)}, f32[192,128]{1,0:T(8,128)S(1)}, u32[]{:S(2)}, u32[]{:S(2)}) %collective-permute-start.10) | collective-permute-done | bytes 98336 | tf_op jit(solution)/shard_map/ppermute | solution.py:544
  85.9 3.5 %collective-permute-start.11 = (f32[192,128]{1,0:T(8,128)S(1)}, f32[192,128]{1,0:T(8,128)S(1)}, u32[]{:S(2)}, u32[]{:S(2)}) collective-permute-start(f32[192,128]{1,0:T(8,128)S(1)} %add.29), channel_id=1, source_target_pairs={{0,1},{1,0},{2,3},{3,2},{4,5},{5,4},{6,7},{7,6},{8,9},{9,8},{10,11... | collective-permute-start | bytes 294920 | tf_op jit(solution)/shard_map/ppermute | solution.py:544
  89.5 0.0 collective-permute-done.12
  89.5 0.7 fusion.3
  90.2 0.2 collective-permute-done.11
  90.4 0.0 copy-done.2
  90.5 0.0 copy-done.3
  90.5 0.7 pad_maximum_fusion.2.summed
  91.2 28.7 %shard_map.141 = (f32[1024,384]{1,0:T(8,128)}, f32[3,512,32]{2,1,0:T(8,128)}) custom-call(s32[2]{0:T(128)} %pad_add_fusion.place, f32[3,512,32]{2,1,0:T(8,128)} %bitcast.36, f32[384,128]{1,0:T(8,128)} %pad_maximum_fusion.2.summed, f32[128,128]{1,0:T(8,128)} %constant.51.clone.factor, f32[32,512]{1,0:T(8,128)} %constant.43.clone.bx, ...), custom_call_target="tpu_custom_call" | custom-call | flops 28000000000 | bytes 84000000 | tf_op jit(solution)/shard_map/pallas_call | solution.py:699
  (10 shorter events, 0.2 us)
Async XLA Ops:
  0.6 4.7 %copy-start.1 = (f32[32,32,384]{2,1,0:T(8,128)S(1)}, f32[32,32,384]{2,1,0:T(8,128)}, u32[]{:S(2)}) copy-start(f32[32,32,384]{2,1,0:T(8,128)} %param.13) | copy-start | bytes 4718596
  2.6 2.7 %copy-start = (f32[32,32,384]{2,1,0:T(8,128)S(1)}, f32[32,32,384]{2,1,0:T(8,128)}, u32[]{:S(2)}) copy-start(f32[32,32,384]{2,1,0:T(8,128)} %param.12) | copy-start | bytes 4718596
  2.6 9.8 %collective-permute-start = (f32[32,32,128]{2,1,0:T(8,128)}, f32[32,32,128]{2,1,0:T(8,128)}, u32[]{:S(2)}, u32[]{:S(2)}) collective-permute-start(f32[32,32,128]{2,1,0:T(8,128)} %constant_dynamic-slice_fusion.1), channel_id=1, source_target_pairs={{0,1},{1,0},{2,3},{3,2},{4,5},{5,4},{6,7},{7,6},{8,9},{9,8},{10,11... | collective-permute-start | bytes 1572872 | tf_op jit(solution)/shard_map/ppermute | solution.py:544
  5.2 7.3 %collective-permute-start.1 = (f32[32,32,128]{2,1,0:T(8,128)}, f32[32,32,128]{2,1,0:T(8,128)}, u32[]{:S(2)}, u32[]{:S(2)}) collective-permute-start(f32[32,32,128]{2,1,0:T(8,128)} %constant_dynamic-slice_fusion), channel_id=1, source_target_pairs={{0,1},{1,0},{2,3},{3,2},{4,5},{5,4},{6,7},{7,6},{8,9},{9,8},{10,11... | collective-permute-start | bytes 1572872 | tf_op jit(solution)/shard_map/ppermute | solution.py:544
  5.5 31.0 %collective-permute-start.2 = (f32[288,384]{1,0:T(8,128)S(1)}, f32[288,384]{1,0:T(8,128)}, u32[]{:S(2)}, u32[]{:S(2)}) collective-permute-start(f32[288,384]{1,0:T(8,128)S(1)} %pad_maximum_fusion), channel_id=1, source_target_pairs={{0,2},{2,4},{4,6},{6,8},{8,10},{10,12},{12,14},{1,3},{3,5},{5,7},{... | collective-permute-start | bytes 1327112 | tf_op jit(solution)/shard_map/ppermute | solution.py:583
  8.7 27.8 %collective-permute-start.3 = (f32[288,384]{1,0:T(8,128)S(1)}, f32[288,384]{1,0:T(8,128)}, u32[]{:S(2)}, u32[]{:S(2)}) collective-permute-start(f32[288,384]{1,0:T(8,128)S(1)} %pad_maximum_fusion.1), channel_id=1, source_target_pairs={{2,0},{4,2},{6,4},{8,6},{10,8},{12,10},{14,12},{3,1},{5,3},{7,5},{... | collective-permute-start | bytes 1327112 | tf_op jit(solution)/shard_map/ppermute | solution.py:584
  38.6 7.4 %collective-permute-start.4 = (f32[512,128]{1,0:T(8,128)S(1)}, f32[512,128]{1,0:T(8,128)S(1)}, u32[]{:S(2)}, u32[]{:S(2)}) collective-permute-start(f32[512,128]{1,0:T(8,128)S(1)} %fusion.1), channel_id=1, source_target_pairs={{0,1},{1,0},{2,3},{3,2},{4,5},{5,4},{6,7},{7,6},{8,9},{9,8},{10,11... | collective-permute-start | bytes 786440 | tf_op jit(solution)/shard_map/ppermute | solution.py:544
  39.6 29.8 %collective-permute-start.5 = (f32[256,384]{1,0:T(8,128)S(1)}, f32[256,384]{1,0:T(8,128)S(1)}, u32[]{:S(2)}, u32[]{:S(2)}) collective-permute-start(f32[256,384]{1,0:T(8,128)S(1)} %get-tuple-element.28), channel_id=1, source_target_pairs={{0,2},{2,4},{4,6},{6,8},{8,10},{10,12},{12,14},{1,3},{3,5},{5,7},{... | collective-permute-start | bytes 1179656 | tf_op jit(solution)/shard_map/ppermute | solution.py:583
  42.6 26.8 %collective-permute-start.6 = (f32[256,384]{1,0:T(8,128)S(1)}, f32[256,384]{1,0:T(8,128)S(1)}, u32[]{:S(2)}, u32[]{:S(2)}) collective-permute-start(f32[256,384]{1,0:T(8,128)S(1)} %get-tuple-element.29), channel_id=1, source_target_pairs={{2,0},{4,2},{6,4},{8,6},{10,8},{12,10},{14,12},{3,1},{5,3},{7,5},{... | collective-permute-start | bytes 1179656 | tf_op jit(solution)/shard_map/ppermute | solution.py:584
  69.4 21.0 %copy-start.2 = (f32[256,384]{1,0:T(8,128)}, f32[256,384]{1,0:T(8,128)S(1)}, u32[]{:S(2)}) copy-start(f32[256,384]{1,0:T(8,128)S(1)} %collective-permute-done.5.rest_1_) | copy-start | bytes 1179652
  69.4 21.0 %copy-start.3 = (f32[256,384]{1,0:T(8,128)}, f32[256,384]{1,0:T(8,128)S(1)}, u32[]{:S(2)}) copy-start(f32[256,384]{1,0:T(8,128)S(1)} %collective-permute-done.6.rest_2_) | copy-start | bytes 1179652
  70.5 1.5 %collective-permute-start.7 = (f32[192,128]{1,0:T(8,128)S(1)}, f32[192,128]{1,0:T(8,128)S(1)}, u32[]{:S(2)}, u32[]{:S(2)}) collective-permute-start(f32[192,128]{1,0:T(8,128)S(1)} %dynamic-slice_bitcast_fusion), channel_id=1, source_target_pairs={{0,1},{1,0},{2,3},{3,2},{4,5},{5,4},{6,7},{7,6},{8,9},{9,8},{10,11... | collective-permute-start | bytes 294920 | tf_op jit(solution)/shard_map/ppermute | solution.py:544
  72.9 4.1 %collective-permute-start.8 = (f32[192,128]{1,0:T(8,128)S(1)}, f32[192,128]{1,0:T(8,128)S(1)}, u32[]{:S(2)}, u32[]{:S(2)}) collective-permute-start(f32[192,128]{1,0:T(8,128)S(1)} %bitcast_add_fusion), channel_id=1, source_target_pairs={{0,2},{2,0},{4,6},{6,4},{8,10},{10,8},{12,14},{14,12},{1,3},{3,1},... | collective-permute-start | bytes 294920 | tf_op jit(solution)/shard_map/ppermute | solution.py:544
  73.2 16.3 %collective-permute-start.12 = (f32[512,128]{1,0:T(8,128)S(1)}, f32[512,128]{1,0:T(8,128)S(1)}, u32[]{:S(2)}, u32[]{:S(2)}) collective-permute-start(f32[512,128]{1,0:T(8,128)S(1)} %fusion), channel_id=1, source_target_pairs={{0,1},{1,0},{2,3},{3,2},{4,5},{5,4},{6,7},{7,6},{8,9},{9,8},{10,11... | collective-permute-start | bytes 786440 | tf_op jit(solution)/shard_map/ppermute | solution.py:544
  77.0 3.5 %collective-permute-start.9 = (f32[192,128]{1,0:T(8,128)S(1)}, f32[192,128]{1,0:T(8,128)S(1)}, u32[]{:S(2)}, u32[]{:S(2)}) collective-permute-start(f32[192,128]{1,0:T(8,128)S(1)} %add.27), channel_id=1, source_target_pairs={{0,4},{2,6},{4,0},{6,2},{8,12},{10,14},{12,8},{14,10},{1,5},{3,7},... | collective-permute-start | bytes 294920 | tf_op jit(solution)/shard_map/ppermute | solution.py:544
  80.5 5.4 %collective-permute-start.10 = (f32[192,128]{1,0:T(8,128)S(1)}, f32[192,128]{1,0:T(8,128)S(1)}, u32[]{:S(2)}, u32[]{:S(2)}) collective-permute-start(f32[192,128]{1,0:T(8,128)S(1)} %add.28), channel_id=1, source_target_pairs={{0,8},{2,10},{4,12},{6,14},{8,0},{10,2},{12,4},{14,6},{1,9},{3,11}... | collective-permute-start | bytes 294920 | tf_op jit(solution)/shard_map/ppermute | solution.py:544
  85.9 4.5 %collective-permute-start.11 = (f32[192,128]{1,0:T(8,128)S(1)}, f32[192,128]{1,0:T(8,128)S(1)}, u32[]{:S(2)}, u32[]{:S(2)}) collective-permute-start(f32[192,128]{1,0:T(8,128)S(1)} %add.29), channel_id=1, source_target_pairs={{0,1},{1,0},{2,3},{3,2},{4,5},{5,4},{6,7},{7,6},{8,9},{9,8},{10,11... | collective-permute-start | bytes 294920 | tf_op jit(solution)/shard_map/ppermute | solution.py:544

commit v3 on v2

--- a/solution.py
+++ b/solution.py
@@ -495,10 +495,10 @@
 
 
 def outer_kernel(n, place, speed_in, field_in, spare_in, image_in, spread, gather, bx_t, *rest):
-    by_t, bz_p, low, high, side_low, side_high, packed, end, *rest = rest
+    by_t, bz_p, low, high, side_low, side_high, kept, given, end, *rest = rest
     speed, field, spare, image, *rest = rest
     raw, thin, edge, f_high, f_low, total, by_own, bz_own, *rest = rest
-    sems_h, sems_e, sems_o, sems_t, sems_s, sems_f = rest
+    sems_h, sems_e, sems_o, sems_t, sems_s, sems_f, packed = rest
     pulls = started(halo_copies(n, low, high, side_low, side_high, thin, sems_h))
     speeds = started(edge_rows(n, speed_in, speed, sems_s))
     fields = started(block_rows(n, (field_in, spare_in), (field, spare), sems_f))
@@ -516,17 +516,24 @@
     force(n, field, image, f_high, f_low)
     waited(tables)
     project(n, f_high, f_low, bz_own, bx_t, by_own, total, packed)
+    half = packed.shape[0] // 2
+    side = place[1] % 2
+    kept[...] = packed[pl.ds(pl.multiple_of(side * half, half), half), :]
+    given[...] = packed[pl.ds(pl.multiple_of((1 - side) * half, half), half), :]
     waited(pushes)
 
 
-def last_kernel(n, place, modes, summed, factor, bx, by, bz_e, spread, gather, *rest):
+def last_kernel(n, place, modes, kept, other, factor, bx, by, bz_e, spread, gather, *rest):
     image, low, high, side_low, side_high, end, updated, *rest = rest
     speed, field, spare, raw, thin, w, by_own, bz_own, sems_h, sems_o, sems_t, sems_f = rest
     tables = started(table_copies(place, ((by, 0, by_own), (bz_e, 1, bz_own)), sems_t))
     pulls = started(halo_copies(n, low, high, side_low, side_high, thin, sems_h))
     images = started(block_rows(n, (image,), (field,), sems_f))
     scale = jnp.concatenate([factor[...]] * 3, axis=0)
-    packed = scale * summed[...]
+    even = place[1] % 2 == 0
+    first = jnp.where(even, kept[...], other[...])
+    second = jnp.where(even, other[...], kept[...])
+    packed = scale * jnp.concatenate([first, second], axis=0)
     coeffs = [own_modes(n, modes, c) + unpacked(packed, c, n) for c in range(3)]
     for c in range(3):
         updated[c] = coeffs[c][:, : n.modes]
@@ -544,23 +551,19 @@
     return lax.ppermute(value, axis, [(i, i ^ step) for i in range(count)])
 
 
-def sum_over_devices(packed):
+def sum_over_devices(kept, given):
     count_height, count_depth = lax.axis_size("ha"), lax.axis_size("dev")
     if count_depth != 2 or count_height & (count_height - 1):
-        return lax.psum(packed, ("ha", "dev"))
-    halves = packed.reshape(2, -1, LANES)
-    side = lax.axis_index("dev")
-    kept = lax.dynamic_index_in_dim(halves, side, 0, False)
-    given = lax.dynamic_index_in_dim(halves, 1 - side, 0, False)
+        even = lax.axis_index("dev") % 2 == 0
+        halves = jnp.stack([jnp.where(even, kept, given), jnp.where(even, given, kept)])
+        halves = lax.psum(halves, ("ha", "dev"))
+        return jnp.where(even, halves[0], halves[1]), jnp.where(even, halves[1], halves[0])
     kept = kept + swap_with(given, "dev", 1)
     step = 1
     while step < count_height:
         kept = kept + swap_with(kept, "ha", step)
         step *= 2
-    other = swap_with(kept, "dev", 1)
-    first = jnp.where(side == 0, kept, other)
-    second = jnp.where(side == 0, other, kept)
-    return jnp.concatenate([first, second], axis=0)
+    return kept, swap_with(kept, "dev", 1)
 
 
 def beside(cells):
@@ -661,12 +664,13 @@
     corner_a = corners(low_a, high_a, thin_count)
     low_b, high_b = to_neighbours(last_b, first_b)
 
-    packed, adjoint_end = pl.pallas_call(
+    kept, given, adjoint_end = pl.pallas_call(
         functools.partial(outer_kernel, n),
         in_specs=[small] + [outside] * 4 + [held] * 3 + [outside] * 6,
-        out_specs=[held, outside],
+        out_specs=[held, held, outside],
         out_shape=[
-            jax.ShapeDtypeStruct((3 * n.chunk, LANES), F32),
+            jax.ShapeDtypeStruct((3 * n.chunk // 2, LANES), F32),
+            jax.ShapeDtypeStruct((3 * n.chunk // 2, LANES), F32),
             jax.ShapeDtypeStruct(flat, F32),
         ],
         scratch_shapes=[
@@ -686,6 +690,7 @@
             semaphores((2,)),
             semaphores((2, 4)),
             semaphores((3,)),
+            pltpu.VMEM((3 * n.chunk, LANES), F32),
         ],
         compiler_params=params(60),
         cost_estimate=cost(16),
@@ -693,12 +698,12 @@
         place, speed, field, spare, image, t["spread"], t["gather"], t["bx_t"], t["by_t"], t["bz_p"],
         low_a, high_a, *corner_a,
     )
-    packed, low_b, high_b = lax.optimization_barrier((packed, low_b, high_b))
-    summed = sum_over_devices(packed)
+    kept, given, low_b, high_b = lax.optimization_barrier((kept, given, low_b, high_b))
+    kept, other = sum_over_devices(kept, given)
     corner_b = corners(low_b, high_b, thin_count)
     image_end, updated = pl.pallas_call(
         functools.partial(last_kernel, n),
-        in_specs=[small, held, held, held, held, outside, outside, held, held] + [outside] * 5,
+        in_specs=[small] + [held] * 5 + [outside, outside, held, held] + [outside] * 5,
         out_specs=[outside, held],
         out_shape=[
             jax.ShapeDtypeStruct(flat, F32),
@@ -720,7 +725,7 @@
         compiler_params=params(60),
         cost_estimate=cost(28),
     )(
-        place, modes, summed, t["factor"], t["bx"], t["by"], t["bz_e"], t["spread"], t["gather"],
+        place, modes, kept, other, t["factor"], t["bx"], t["by"], t["bz_e"], t["spread"], t["gather"],
         image, low_b, high_b, *corner_b,
     )
     return (

time: 121 us -> 121 us (level)
    reshape x2, local copies, waits for them, and re-layouts: 0.1 us -> 2.1 us  [rows_sent(): return cells.reshape(-1, depth)]
    dynamic_slice x2, local copies, waits for them, and re-layouts: 3.86 us -> 2.27 us  [beside(): lax.dynamic_slice_in_dim(cells, start, LANES, cells.ndim - 1)]
where the time goes in v3:
time: 121 us; the launch traced here: 120 us
  Pallas kernels  76 us (63%)
  starting transfers between devices  20 us (17%)
  waiting for transfers between devices  13 us (11%)
  local copies, waits for them, and re-layouts  8.65 us (7%)
  other arithmetic  1.65 us (1%)
    pallas_call x1, Pallas kernels, per_device(): pl.pallas_call(functools.partial(last_kernel, n), in_specs=[small] + [hel...  29.3 us
    pallas_call x1, Pallas kernels, per_device(): pl.pallas_call(functools.partial(inner_kernel, n), in_specs=[small, held,...  24 us
    pallas_call x1, Pallas kernels, per_device(): pl.pallas_call(functools.partial(outer_kernel, n), in_specs=[small] + [ou...  22.7 us
    ppermute x9, waiting for transfers between devices, swap_with(): return lax.ppermute(value, axis, [(i, i ^ step) for i in range(count)])  13 us
    ppermute x9, starting transfers between devices, swap_with(): return lax.ppermute(value, axis, [(i, i ^ step) for i in range(count)])  7.48 us
    ppermute x2, starting transfers between devices, to_neighbours(): high = lax.ppermute(first_rows, 'ha', [(i + 1, i) for i in ends])  6.39 us
    ppermute x2, starting transfers between devices, to_neighbours(): low = lax.ppermute(last_rows, 'ha', [(i, i + 1) for i in ends])  6.14 us
  transfers between devices with their start and end apart: 13, of which 5 were waited for; matrix products, arithmetic and copies ran while one was open for 4% of the time, Pallas kernels for 39%

profile of v3, /device:TPU:25, one launch (start us, length us, event | category | flops | bytes accessed | tf_op | source)
XLA Modules:
  0.0 120.4 jit_solution(18162003735977674161)
XLA Ops:
  0.6 0.0 copy-start
  0.7 1.2 constant_dynamic-slice_fusion
  1.8 0.7 collective-permute-start.1
  2.6 1.1 constant_dynamic-slice_fusion.1
  3.7 0.1 collective-permute-start
  3.8 0.0 copy-done
  3.8 0.1 fusion.2
  3.8 1.2 slice_bitcast_fusion.2
  5.1 3.1 %collective-permute-start.2 = (f32[288,384]{1,0:T(8,128)S(1)}, f32[288,384]{1,0:T(8,128)}, u32[]{:S(2)}, u32[]{:S(2)}) collective-permute-start(f32[288,384]{1,0:T(8,128)S(1)} %pad_maximum_fusion), channel_id=1, source_target_pairs={{0,2},{2,4},{4,6},{6,8},{8,10},{10,12},{12,14},{1,3},{3,5},{5,7},{... | collective-permute-start | bytes 1327112 | tf_op jit(solution)/shard_map/ppermute | solution.py:586
  8.3 3.0 %collective-permute-start.3 = (f32[288,384]{1,0:T(8,128)S(1)}, f32[288,384]{1,0:T(8,128)}, u32[]{:S(2)}, u32[]{:S(2)}) collective-permute-start(f32[288,384]{1,0:T(8,128)S(1)} %pad_maximum_fusion.1), channel_id=1, source_target_pairs={{2,0},{4,2},{6,4},{8,6},{10,8},{12,10},{14,12},{3,1},{5,3},{7,5},{... | collective-permute-start | bytes 1327112 | tf_op jit(solution)/shard_map/ppermute | solution.py:587
  11.3 0.6 pad_add_fusion.place
  11.9 0.9 slice_bitcast_fusion
  12.8 0.0 collective-permute-done.1
  12.8 0.0 collective-permute-done
  12.8 24.0 %shard_map.139 = (f32[4,48,4,4,8,128]{5,4,3,2,1,0:T(8,128)}, f32[48,4,4,8,128]{4,3,2,1,0:T(8,128)}, f32[48,4,4,8,128]{4,3,2,1,0:T(8,128)}, f32[48,4,4,8,128]{4,3,2,1,0:T(8,128)}) custom-call(s32[2]{0:T(128)} %pad_add_fusion.place, f32[3,512,32]{2,1,0:T(8,128)} %bitcast.28, f32[32,512]{1,0:T(8,128)} %constant.32.clone.bx, f32[8,48,512]{2,1,0:T(8,128)} %constant.33.clone.by, ...), custom_call_target="tpu_custom_call" | custom-call | flops 20000000000 | bytes 60000000 | tf_op jit(solution)/shard_map/pallas_call | solution.py:644
  36.8 0.0 copy-start.4
  36.8 0.0 copy-start.3
  36.9 0.0 collective-permute-done.2.rest_2_
  36.9 0.0 collective-permute-done.3.rest_3_
  36.9 1.1 slice.42
  38.0 1.0 slice.43
  39.0 1.1 collective-permute-start.4
  40.1 0.0 copy-done.4
  40.1 3.0 %collective-permute-start.5 = (f32[256,384]{1,0:T(8,128)S(1)}, f32[256,384]{1,0:T(8,128)S(1)}, u32[]{:S(2)}, u32[]{:S(2)}) collective-permute-start(f32[256,384]{1,0:T(8,128)S(1)} %copy-done.4), channel_id=1, source_target_pairs={{0,2},{2,4},{4,6},{6,8},{8,10},{10,12},{12,14},{1,3},{3,5},{5,7},{... | collective-permute-start | bytes 1179656 | tf_op jit(solution)/shard_map/ppermute | solution.py:586
  43.1 0.0 copy-done.3
  43.1 3.4 %collective-permute-start.6 = (f32[256,384]{1,0:T(8,128)S(1)}, f32[256,384]{1,0:T(8,128)S(1)}, u32[]{:S(2)}, u32[]{:S(2)}) collective-permute-start(f32[256,384]{1,0:T(8,128)S(1)} %copy-done.3), channel_id=1, source_target_pairs={{2,0},{4,2},{6,4},{8,6},{10,8},{12,10},{14,12},{3,1},{5,3},{7,5},{... | collective-permute-start | bytes 1179656 | tf_op jit(solution)/shard_map/ppermute | solution.py:587
  46.5 0.0 collective-permute-done.4
  46.5 0.7 fusion.4
  47.2 22.7 %shard_map.140 = (f32[192,128]{1,0:T(8,128)}, f32[192,128]{1,0:T(8,128)}, f32[1024,384]{1,0:T(8,128)}) custom-call(s32[2]{0:T(128)} %pad_add_fusion.place, f32[4,48,4,4,8,128]{5,4,3,2,1,0:T(8,128)} %get-tuple-element.21.speed_in, f32[48,4,4,8,128]{4,3,2,1,0:T(8,128)} %get-tuple-element.23.field_in, f32[48,4,4,8,128]{4,3,2,1,0:T(8,128)} %get-tuple-element.24.spare_in, ...), custom_call_target="tpu_custom_call" | custom-call | flops 16000000000 | bytes 48000000 | tf_op jit(solution)/shard_map/pallas_call | solution.py:667
  70.0 0.0 collective-permute-done.5.rest_1_
  70.0 0.0 copy-start.1
  70.0 0.0 collective-permute-done.6.rest_2_
  70.0 0.0 copy-start.2
  70.0 0.7 collective-permute-start.7
  70.7 1.2 collective-permute-done.7
  71.8 0.9 add.16
  72.7 0.3 collective-permute-start.8
  73.0 0.7 collective-permute-start.12
  73.7 3.1 %collective-permute-done.8 = f32[192,128]{1,0:T(8,128)S(1)} collective-permute-done((f32[192,128]{1,0:T(8,128)S(1)}, f32[192,128]{1,0:T(8,128)S(1)}, u32[]{:S(2)}, u32[]{:S(2)}) %collective-permute-start.8) | collective-permute-done | bytes 98336 | tf_op jit(solution)/shard_map/ppermute | solution.py:551
  76.8 0.2 collective-permute-start.9
  77.1 3.3 %collective-permute-done.9 = f32[192,128]{1,0:T(8,128)S(1)} collective-permute-done((f32[192,128]{1,0:T(8,128)S(1)}, f32[192,128]{1,0:T(8,128)S(1)}, u32[]{:S(2)}, u32[]{:S(2)}) %collective-permute-start.9) | collective-permute-done | bytes 98336 | tf_op jit(solution)/shard_map/ppermute | solution.py:551
  80.4 0.1 collective-permute-start.10
  80.5 5.3 %collective-permute-done.10 = f32[192,128]{1,0:T(8,128)S(1)} collective-permute-done((f32[192,128]{1,0:T(8,128)S(1)}, f32[192,128]{1,0:T(8,128)S(1)}, u32[]{:S(2)}, u32[]{:S(2)}) %collective-permute-start.10) | collective-permute-done | bytes 98336 | tf_op jit(solution)/shard_map/ppermute | solution.py:551
  85.8 0.0 copy-start.5
  85.8 3.5 %collective-permute-start.11 = (f32[192,128]{1,0:T(8,128)S(1)}, f32[192,128]{1,0:T(8,128)S(1)}, u32[]{:S(2)}, u32[]{:S(2)}) collective-permute-start(f32[192,128]{1,0:T(8,128)S(1)} %add.19.kept), channel_id=1, source_target_pairs={{0,1},{1,0},{2,3},{3,2},{4,5},{5,4},{6,7},{7,6},{8,9},{9,8},{10,11... | collective-permute-start | bytes 294920 | tf_op jit(solution)/shard_map/ppermute | solution.py:551
  89.3 0.0 collective-permute-done.12
  89.3 0.7 fusion.3
  90.1 0.2 collective-permute-done.11.other
  90.3 0.0 copy-start.6
  90.3 0.0 copy-done.1
  90.3 0.0 copy-done.2
  90.3 0.0 copy-done.5
  90.3 0.6 copy-done.6
  90.9 29.3 %shard_map.141 = (f32[1024,384]{1,0:T(8,128)}, f32[3,512,32]{2,1,0:T(8,128)}) custom-call(s32[2]{0:T(128)} %pad_add_fusion.place, f32[3,512,32]{2,1,0:T(8,128)} %bitcast.29, f32[192,128]{1,0:T(8,128)} %copy-done.5, f32[192,128]{1,0:T(8,128)} %copy-done.6, f32[128,128]{1,0:T(8,128)} %constant.40.clone.factor, f32[32,512]{1,0:T(8,128)} %constant.32.clone.bx, ...), custom_call_target="tpu_custom_call" | custom-call | flops 28000000000 | bytes 84000000 | tf_op jit(solution)/shard_map/pallas_call | solution.py:704
  (9 shorter events, 0.2 us)
Async XLA Ops:
  0.6 3.1 %copy-start = (f32[32,32,384]{2,1,0:T(8,128)S(1)}, f32[32,32,384]{2,1,0:T(8,128)}, u32[]{:S(2)}) copy-start(f32[32,32,384]{2,1,0:T(8,128)} %param.12) | copy-start | bytes 4718596
  1.8 11.0 %collective-permute-start.1 = (f32[32,32,128]{2,1,0:T(8,128)S(1)}, f32[32,32,128]{2,1,0:T(8,128)}, u32[]{:S(2)}, u32[]{:S(2)}) collective-permute-start(f32[32,32,128]{2,1,0:T(8,128)S(1)} %constant_dynamic-slice_fusion), channel_id=1, source_target_pairs={{0,1},{1,0},{2,3},{3,2},{4,5},{5,4},{6,7},{7,6},{8,9},{9,8},{10,11... | collective-permute-start | bytes 1572872 | tf_op jit(solution)/shard_map/ppermute | solution.py:551
  3.7 9.2 %collective-permute-start = (f32[32,32,128]{2,1,0:T(8,128)S(1)}, f32[32,32,128]{2,1,0:T(8,128)}, u32[]{:S(2)}, u32[]{:S(2)}) collective-permute-start(f32[32,32,128]{2,1,0:T(8,128)S(1)} %constant_dynamic-slice_fusion.1), channel_id=1, source_target_pairs={{0,1},{1,0},{2,3},{3,2},{4,5},{5,4},{6,7},{7,6},{8,9},{9,8},{10,11... | collective-permute-start | bytes 1572872 | tf_op jit(solution)/shard_map/ppermute | solution.py:551
  5.1 31.8 %collective-permute-start.2 = (f32[288,384]{1,0:T(8,128)S(1)}, f32[288,384]{1,0:T(8,128)}, u32[]{:S(2)}, u32[]{:S(2)}) collective-permute-start(f32[288,384]{1,0:T(8,128)S(1)} %pad_maximum_fusion), channel_id=1, source_target_pairs={{0,2},{2,4},{4,6},{6,8},{8,10},{10,12},{12,14},{1,3},{3,5},{5,7},{... | collective-permute-start | bytes 1327112 | tf_op jit(solution)/shard_map/ppermute | solution.py:586
  8.3 28.6 %collective-permute-start.3 = (f32[288,384]{1,0:T(8,128)S(1)}, f32[288,384]{1,0:T(8,128)}, u32[]{:S(2)}, u32[]{:S(2)}) collective-permute-start(f32[288,384]{1,0:T(8,128)S(1)} %pad_maximum_fusion.1), channel_id=1, source_target_pairs={{2,0},{4,2},{6,4},{8,6},{10,8},{12,10},{14,12},{3,1},{5,3},{7,5},{... | collective-permute-start | bytes 1327112 | tf_op jit(solution)/shard_map/ppermute | solution.py:587
  36.8 3.3 %copy-start.4 = (f32[256,384]{1,0:T(8,128)S(1)}, f32[256,384]{1,0:T(8,128)}, u32[]{:S(2)}) copy-start(f32[256,384]{1,0:T(8,128)} %get-tuple-element.31) | copy-start | bytes 1179652
  36.8 6.3 %copy-start.3 = (f32[256,384]{1,0:T(8,128)S(1)}, f32[256,384]{1,0:T(8,128)}, u32[]{:S(2)}) copy-start(f32[256,384]{1,0:T(8,128)} %get-tuple-element.32) | copy-start | bytes 1179652
  39.0 7.5 %collective-permute-start.4 = (f32[512,128]{1,0:T(8,128)S(1)}, f32[512,128]{1,0:T(8,128)S(1)}, u32[]{:S(2)}, u32[]{:S(2)}) collective-permute-start(f32[512,128]{1,0:T(8,128)S(1)} %fusion.1), channel_id=1, source_target_pairs={{0,1},{1,0},{2,3},{3,2},{4,5},{5,4},{6,7},{7,6},{8,9},{9,8},{10,11... | collective-permute-start | bytes 786440 | tf_op jit(solution)/shard_map/ppermute | solution.py:551
  40.1 29.8 %collective-permute-start.5 = (f32[256,384]{1,0:T(8,128)S(1)}, f32[256,384]{1,0:T(8,128)S(1)}, u32[]{:S(2)}, u32[]{:S(2)}) collective-permute-start(f32[256,384]{1,0:T(8,128)S(1)} %copy-done.4), channel_id=1, source_target_pairs={{0,2},{2,4},{4,6},{6,8},{8,10},{10,12},{12,14},{1,3},{3,5},{5,7},{... | collective-permute-start | bytes 1179656 | tf_op jit(solution)/shard_map/ppermute | solution.py:586
  43.1 26.8 %collective-permute-start.6 = (f32[256,384]{1,0:T(8,128)S(1)}, f32[256,384]{1,0:T(8,128)S(1)}, u32[]{:S(2)}, u32[]{:S(2)}) collective-permute-start(f32[256,384]{1,0:T(8,128)S(1)} %copy-done.3), channel_id=1, source_target_pairs={{2,0},{4,2},{6,4},{8,6},{10,8},{12,10},{14,12},{3,1},{5,3},{7,5},{... | collective-permute-start | bytes 1179656 | tf_op jit(solution)/shard_map/ppermute | solution.py:587
  70.0 20.3 %copy-start.1 = (f32[256,384]{1,0:T(8,128)}, f32[256,384]{1,0:T(8,128)S(1)}, u32[]{:S(2)}) copy-start(f32[256,384]{1,0:T(8,128)S(1)} %collective-permute-done.5.rest_1_) | copy-start | bytes 1179652
  70.0 20.3 %copy-start.2 = (f32[256,384]{1,0:T(8,128)}, f32[256,384]{1,0:T(8,128)S(1)}, u32[]{:S(2)}) copy-start(f32[256,384]{1,0:T(8,128)S(1)} %collective-permute-done.6.rest_2_) | copy-start | bytes 1179652
  70.0 1.8 %collective-permute-start.7 = (f32[192,128]{1,0:T(8,128)}, f32[192,128]{1,0:T(8,128)S(1)}, u32[]{:S(2)}, u32[]{:S(2)}) collective-permute-start(f32[192,128]{1,0:T(8,128)} %get-tuple-element.34), channel_id=1, source_target_pairs={{0,1},{1,0},{2,3},{3,2},{4,5},{5,4},{6,7},{7,6},{8,9},{9,8},{10,11... | collective-permute-start | bytes 294920 | tf_op jit(solution)/shard_map/ppermute | solution.py:551
  72.7 4.1 %collective-permute-start.8 = (f32[192,128]{1,0:T(8,128)S(1)}, f32[192,128]{1,0:T(8,128)S(1)}, u32[]{:S(2)}, u32[]{:S(2)}) collective-permute-start(f32[192,128]{1,0:T(8,128)S(1)} %add.16), channel_id=1, source_target_pairs={{0,2},{2,0},{4,6},{6,4},{8,10},{10,8},{12,14},{14,12},{1,3},{3,1},... | collective-permute-start | bytes 294920 | tf_op jit(solution)/shard_map/ppermute | solution.py:551
  73.0 16.3 %collective-permute-start.12 = (f32[512,128]{1,0:T(8,128)S(1)}, f32[512,128]{1,0:T(8,128)S(1)}, u32[]{:S(2)}, u32[]{:S(2)}) collective-permute-start(f32[512,128]{1,0:T(8,128)S(1)} %fusion), channel_id=1, source_target_pairs={{0,1},{1,0},{2,3},{3,2},{4,5},{5,4},{6,7},{7,6},{8,9},{9,8},{10,11... | collective-permute-start | bytes 786440 | tf_op jit(solution)/shard_map/ppermute | solution.py:551
  76.8 3.5 %collective-permute-start.9 = (f32[192,128]{1,0:T(8,128)S(1)}, f32[192,128]{1,0:T(8,128)S(1)}, u32[]{:S(2)}, u32[]{:S(2)}) collective-permute-start(f32[192,128]{1,0:T(8,128)S(1)} %add.17), channel_id=1, source_target_pairs={{0,4},{2,6},{4,0},{6,2},{8,12},{10,14},{12,8},{14,10},{1,5},{3,7},... | collective-permute-start | bytes 294920 | tf_op jit(solution)/shard_map/ppermute | solution.py:551
  80.4 5.4 %collective-permute-start.10 = (f32[192,128]{1,0:T(8,128)S(1)}, f32[192,128]{1,0:T(8,128)S(1)}, u32[]{:S(2)}, u32[]{:S(2)}) collective-permute-start(f32[192,128]{1,0:T(8,128)S(1)} %add.18), channel_id=1, source_target_pairs={{0,8},{2,10},{4,12},{6,14},{8,0},{10,2},{12,4},{14,6},{1,9},{3,11}... | collective-permute-start | bytes 294920 | tf_op jit(solution)/shard_map/ppermute | solution.py:551
  85.8 4.5 %copy-start.5 = (f32[192,128]{1,0:T(8,128)}, f32[192,128]{1,0:T(8,128)S(1)}, u32[]{:S(2)}) copy-start(f32[192,128]{1,0:T(8,128)S(1)} %add.19.kept) | copy-start | bytes 294916
  85.8 4.5 %collective-permute-start.11 = (f32[192,128]{1,0:T(8,128)S(1)}, f32[192,128]{1,0:T(8,128)S(1)}, u32[]{:S(2)}, u32[]{:S(2)}) collective-permute-start(f32[192,128]{1,0:T(8,128)S(1)} %add.19.kept), channel_id=1, source_target_pairs={{0,1},{1,0},{2,3},{3,2},{4,5},{5,4},{6,7},{7,6},{8,9},{9,8},{10,11... | collective-permute-start | bytes 294920 | tf_op jit(solution)/shard_map/ppermute | solution.py:551
  90.3 0.6 copy-start.6
